TPU v7x, 128 devices: a whole 4x4x4 slice. The times are simulated.
128 devices in a mesh: row: 8 (over y_lo, x), col: 16 (over z, y_hi, core).
Axes of the slice: x: 4, y: 4 (y_hi: 2, y_lo: 2; y = y_hi * 2 + y_lo), z: 4, core: 2. Of those that a mesh axis runs over, the one named last changes fastest.
Arguments:
- design: float32 [16384, 16384], P('row', 'col'), may hold values from -1 to 1
- coefficients: float32 [2, 8], replicated, may hold values from -3 to 3
- focal_steps: int32 [2], replicated, may hold values from 1 to 63, as said below
- target: float32 [2, 128, 128], replicated, may hold values from 0 to 2
Outputs:
- gradient: float32 [16384, 16384], P('row', 'col')
- field: float32 [2, 2, 128, 128], replicated
Inputs may be any that keep to these rules, and one draw needn't show every extreme that they name: `focal_steps`: every chirp rate is odd, and one of them is 63.
All inputs are finite; a program needn't handle non-finite values.
Results may differ from a plain program's by a relative error of at most 0.0073.
Values sent between devices are 32-bit elements; how exact they have to be, the bound alone decides.
A program may use at most 128 MiB of HBM per device.

v0:
```python
import math

import jax
import jax.numpy as jnp
from jax import lax
from jax.sharding import PartitionSpec as P


def chirp_pair(positions, total, step, focal):
    window = jnp.arange(focal, dtype=jnp.int32) + (total // 2 - focal // 2)
    period = 2 * total
    offset = jnp.mod(window[:, None] - positions[None, :], period)
    phase_index = jnp.mod(jnp.mod(offset * offset, period) * step, period)
    angle = jnp.pi * phase_index.astype(jnp.float32) / total
    scale = 1.0 / math.sqrt(total)
    return (
        (jnp.cos(angle) * scale).astype(jnp.bfloat16),
        (jnp.sin(angle) * scale).astype(jnp.bfloat16),
    )


def transmission(design, coefficients):
    t_prev = jnp.ones_like(design)
    t_cur = design
    u_prev = jnp.ones_like(design)
    u_cur = 2.0 * design
    real_part = coefficients[0, 0] + coefficients[0, 1] * design
    imag_part = coefficients[1, 0] + coefficients[1, 1] * design
    real_slope = coefficients[0, 1] * t_prev
    imag_slope = coefficients[1, 1] * t_prev
    for order in range(2, coefficients.shape[1]):
        t_next = 2.0 * design * t_cur - t_prev
        real_part = real_part + coefficients[0, order] * t_next
        imag_part = imag_part + coefficients[1, order] * t_next
        real_slope = real_slope + coefficients[0, order] * order * u_cur
        imag_slope = imag_slope + coefficients[1, order] * order * u_cur
        t_prev, t_cur = (t_cur, t_next)
        u_prev, u_cur = (u_cur, 2.0 * design * u_cur - u_prev)
    return (real_part, imag_part, real_slope, imag_slope)


def exact(left, right):
    return jnp.dot(left, right, precision=lax.Precision.HIGHEST, preferred_element_type=jnp.float32)


def rows_section(row_tables, part_r, part_i):
    fields = []
    for depth in range(len(row_tables)):
        row_r32 = row_tables[depth][0].astype(jnp.float32)
        row_i32 = row_tables[depth][1].astype(jnp.float32)
        field_r = exact(row_r32, part_r[depth]) - exact(row_i32, part_i[depth])
        field_i = exact(row_r32, part_i[depth]) + exact(row_i32, part_r[depth])
        fields.append(jnp.stack([field_r, field_i]))
    return jnp.stack(fields)


def body(design, coefficients, focal_steps, target):
    depths = focal_steps.shape[0]
    focal = target.shape[1]
    loc_rows, loc_cols = design.shape
    total_rows = loc_rows * lax.axis_size("row")
    total_cols = loc_cols * lax.axis_size("col")
    row_pos = lax.axis_index("row") * loc_rows + jnp.arange(loc_rows, dtype=jnp.int32)
    col_pos = lax.axis_index("col") * loc_cols + jnp.arange(loc_cols, dtype=jnp.int32)
    row_tables = [
        chirp_pair(row_pos, total_rows, focal_steps[depth], focal) for depth in range(depths)
    ]
    col_tables = [
        chirp_pair(col_pos, total_cols, focal_steps[depth], focal) for depth in range(depths)
    ]
    real_part, imag_part, real_slope, imag_slope = transmission(design, coefficients)
    real_b = real_part.astype(jnp.bfloat16)
    imag_b = imag_part.astype(jnp.bfloat16)
    right_real = jnp.concatenate(
        [jnp.concatenate([tab[0].T, tab[1].T], axis=1) for tab in col_tables], axis=1
    )
    right_imag = jnp.concatenate(
        [jnp.concatenate([-tab[1].T, tab[0].T], axis=1) for tab in col_tables], axis=1
    )
    partial_value = jnp.dot(real_b, right_real, preferred_element_type=jnp.float32) + jnp.dot(
        imag_b, right_imag, preferred_element_type=jnp.float32
    )
    partial_value = lax.psum(partial_value, "col")
    part_r = [
        partial_value[:, 2 * depth * focal : (2 * depth + 1) * focal] for depth in range(depths)
    ]
    part_i = [
        partial_value[:, (2 * depth + 1) * focal : (2 * depth + 2) * focal]
        for depth in range(depths)
    ]
    field = lax.psum(rows_section(row_tables, part_r, part_i), "row")
    factor = math.sqrt(total_rows * total_cols) / (4.0 * focal)
    excess = field[:, 0] * field[:, 0] + field[:, 1] * field[:, 1] - target
    grad_r = 4.0 * factor * excess * field[:, 0]
    grad_i = 4.0 * factor * excess * field[:, 1]
    backs = []
    rights = []
    for depth in range(depths):
        row_r32 = row_tables[depth][0].astype(jnp.float32).T
        row_i32 = row_tables[depth][1].astype(jnp.float32).T
        back_r = (exact(row_r32, grad_r[depth]) + exact(row_i32, grad_i[depth])).astype(
            jnp.bfloat16
        )
        back_i = (exact(row_i32, grad_r[depth]) - exact(row_r32, grad_i[depth])).astype(
            jnp.bfloat16
        )
        backs.append(jnp.concatenate([back_r, back_i], axis=1))
        col_r, col_i = col_tables[depth]
        rights.append(
            jnp.concatenate(
                [jnp.concatenate([col_r, col_i], axis=1), jnp.concatenate([-col_i, col_r], axis=1)],
                axis=0,
            )
        )
    combined = jnp.dot(
        jnp.concatenate(backs, axis=1),
        jnp.concatenate(rights, axis=0),
        preferred_element_type=jnp.float32,
    )
    gradient = real_slope * combined[:, :loc_cols] - imag_slope * combined[:, loc_cols:]
    return (gradient, field)


def solution(mesh):
    return jax.shard_map(
        body,
        mesh=mesh,
        in_specs=(P("row", "col"), P(), P(), P()),
        out_specs=(P("row", "col"), P()),
        check_vma=False,
    )
```

profile of v0, /device:TPU:0, one launch (start us, length us, event | category | flops | bytes accessed | tf_op | source)
XLA Modules:
  0.0 418.9 jit_solution(11311956759185814794)
XLA Ops:
  8.6 5.9 %fusion.107 = (bf16[1024,128]{1,0:T(8,128)(2,1)S(1)}, bf16[1024,128]{1,0:T(8,128)(2,1)S(1)}) fusion(s32[]{:T(128)} %bitcast.7, s32[1024]{0:T(1024)S(1)} %iota_add_fusion.1, s32[128]{0:T(128)S(1)} %iota_add_fusion.2, s32[]{:T(128)} %bitcast.9), kind=kLoop, calls=%fused_computation.194 | loop fusion | flops 8126464 | bytes 528904 | tf_op jit(solution)/shard_map/neg | solution.py:78
  14.5 6.6 %multiply_convert_fusion.11 = (bf16[1024,128]{1,0:T(8,128)(2,1)S(1)}, bf16[1024,128]{1,0:T(8,128)(2,1)S(1)}, bf16[1024,128]{1,0:T(8,128)(2,1)S(1)}, bf16[1024,128]{1,0:T(8,128)(2,1)S(1)}) fusion(s32[]{:T(128)} %bitcast.7, s32[1024]{0:T(1024)S(1)} %iota_add_fusion.1, s32[128]{0:T(128)S(1)} %iota_add_fusion.2, s32[]{:T(128)} %bitcast.9), kind=kLoop, calls=%fused_computation.177 | loop fusion | flops 7864320 | bytes 1053192 | tf_op jit(solution)/shard_map/convert_element_type | solution.py:17
  23.1 15.5 %fusion.14 = f32[2048,512]{1,0:T(8,128)S(1)} fusion(f32[2048,1024]{1,0:T(8,128)} %param.4, f32[]{:T(128)} %bitcast.6, f32[]{:T(128)} %bitcast.5, f32[]{:T(128)} %bitcast.4, f32[]{:T(128)} %bitcast.3, f32[]{:T(128)} %bitcast.2, f32[]{:T(128)} %bitcast.1, f32[]{:T(128)} %bitcast.8, f32[]{:T(128)} %bitcast, bf16[1024,128]{1,0:T(8,128)(2,1)S(1)} %get-tuple-element.13, ...), kind=kOutput, calls=%fused_computation.29 | convolution fusion | flops 2210398208 | bytes 13631520 | tf_op jit(solution)/shard_map/dot_general | solution.py:80
  38.7 15.5 %fusion.16 = f32[2048,512]{1,0:T(8,128)} fusion(f32[2048,512]{1,0:T(8,128)S(1)} %fusion.14, f32[2048,1024]{1,0:T(8,128)S(1)} %bitcast.61, f32[]{:T(128)} %bitcast.17, f32[]{:T(128)} %bitcast.16, f32[]{:T(128)} %bitcast.15, f32[]{:T(128)} %bitcast.14, f32[]{:T(128)} %bitcast.13, f32[]{:T(128)} %bitcast.12, f32[]{:T(128)} %bitcast.11, f32[]{:T(128)} %bitcast.10, ...), kind=kOutput, calls=%fused_computation.31 | convolution fusion | flops 2211446784 | bytes 17825824 | tf_op jit(solution)/shard_map/dot_general | solution.py:80
  61.9 7.3 %multiply_convert_fusion.6 = (bf16[128,1024]{1,0:T(8,128)(2,1)S(1)}, bf16[128,1024]{1,0:T(8,128)(2,1)S(1)}, bf16[128,1024]{1,0:T(8,128)(2,1)}, bf16[128,1024]{1,0:T(8,128)(2,1)}) fusion(s32[]{:T(128)} %bitcast.7, s32[1024]{0:T(1024)S(1)} %iota_add_fusion.1, s32[128]{0:T(128)S(1)} %iota_add_fusion.2, s32[]{:T(128)} %bitcast.9), kind=kLoop, calls=%fused_computation.172 | loop fusion | flops 7864320 | bytes 1053192 | tf_op jit(solution)/shard_map/convert_element_type | solution.py:18
  69.2 145.2 %all-reduce.3.cloned.1.call-done = f32[2048,512]{1,0:T(8,128)} async-done(((f32[2048,512]{1,0:T(8,128)}), f32[2048,512]{1,0:T(8,128)}) %all-reduce.3.cloned.1.call-update) | async-done | bytes 4194320 | tf_op jit(solution)/shard_map/psum | solution.py:83
  214.5 7.5 %fusion.77 = f32[128,128]{1,0:T(8,128)S(1)} fusion(f32[2048,512]{1,0:T(8,128)} %all-reduce.3.cloned.1.call-done, s32[]{:T(128)} %bitcast.7, s32[2048]{0:T(1024)S(1)} %iota_add_fusion, s32[128]{0:T(128)S(1)} %iota_add_fusion.2), kind=kOutput, calls=%fused_computation.118 | convolution fusion | flops 413138944 | bytes 1123328 | tf_op jit(solution)/shard_map/dot_general | solution.py:43
  227.9 6.0 %fusion.75 = f32[128,128]{1,0:T(8,128)S(1)} fusion(f32[2048,512]{1,0:T(8,128)S(1)} %copy-done.2, s32[]{:T(128)} %bitcast.9, s32[2048]{0:T(1024)S(1)} %iota_add_fusion, s32[128]{0:T(128)S(1)} %iota_add_fusion.2), kind=kOutput, calls=%fused_computation.116 | convolution fusion | flops 413138944 | bytes 1122820 | tf_op jit(solution)/shard_map/dot_general | solution.py:43
  233.9 6.0 %fusion.81 = f32[128,128]{1,0:T(8,128)S(1)} fusion(f32[2048,512]{1,0:T(8,128)S(1)} %copy-done.2, s32[]{:T(128)} %bitcast.7, s32[2048]{0:T(1024)S(1)} %iota_add_fusion, s32[128]{0:T(128)S(1)} %iota_add_fusion.2), kind=kOutput, calls=%fused_computation.122 | convolution fusion | flops 413138944 | bytes 1122820 | tf_op jit(solution)/shard_map/dot_general | solution.py:43
  239.8 6.2 %fusion.46 = f32[1,128,128]{2,1,0:T(8,128)S(1)} fusion(f32[128,128]{1,0:T(8,128)S(1)} %fusion.77, f32[2048,512]{1,0:T(8,128)S(1)} %copy-done.2, s32[]{:T(128)} %bitcast.7, s32[2048]{0:T(1024)S(1)} %iota_add_fusion, s32[128]{0:T(128)S(1)} %iota_add_fusion.2), kind=kOutput, calls=%fused_computation.82 | convolution fusion | flops 413155328 | bytes 1188356 | tf_op jit(solution)/shard_map/dot_general | solution.py:43
  251.9 6.3 %fusion.45 = f32[1,128,128]{2,1,0:T(8,128)S(1)} fusion(f32[128,128]{1,0:T(8,128)S(1)} %fusion.75, f32[2048,512]{1,0:T(8,128)S(1)} %copy-done.2, s32[]{:T(128)} %bitcast.9, s32[2048]{0:T(1024)S(1)} %iota_add_fusion, s32[128]{0:T(128)S(1)} %iota_add_fusion.2), kind=kOutput, calls=%fused_computation.80 | convolution fusion | flops 413155328 | bytes 1188356 | tf_op jit(solution)/shard_map/dot_general | solution.py:43
  258.2 6.0 %fusion.47 = f32[1,128,128]{2,1,0:T(8,128)S(1)} fusion(f32[128,128]{1,0:T(8,128)S(1)} %fusion.81, f32[2048,512]{1,0:T(8,128)S(1)} %copy-done.2, s32[]{:T(128)} %bitcast.7, s32[2048]{0:T(1024)S(1)} %iota_add_fusion, s32[128]{0:T(128)S(1)} %iota_add_fusion.2), kind=kOutput, calls=%fused_computation.84 | convolution fusion | flops 413155328 | bytes 1188356 | tf_op jit(solution)/shard_map/dot_general | solution.py:43
  265.0 6.7 %fusion.109 = (bf16[128,1024]{1,0:T(8,128)(2,1)}, bf16[128,1024]{1,0:T(8,128)(2,1)}) fusion(s32[]{:T(128)} %bitcast.7, s32[1024]{0:T(1024)S(1)} %iota_add_fusion.1, s32[128]{0:T(128)S(1)} %iota_add_fusion.2, s32[]{:T(128)} %bitcast.9), kind=kLoop, calls=%fused_computation.196 | loop fusion | flops 8126464 | bytes 528904 | tf_op jit(solution)/shard_map/neg | solution.py:111
  271.7 66.3 %all-reduce.5.cloned.1.call-done = f32[2,2,128,128]{3,2,1,0:T(8,128)} async-done(((f32[2,2,128,128]{3,2,1,0:T(8,128)}), f32[2,2,128,128]{3,2,1,0:T(8,128)}) %all-reduce.5.cloned.1.call-update) | async-done | bytes 262160 | tf_op jit(solution)/shard_map/psum | solution.py:91
  339.0 5.9 %fusion.104 = f32[2048,128]{1,0:T(8,128)S(1)} fusion(s32[]{:T(128)} %bitcast.9, s32[2048]{0:T(1024)S(1)} %iota_add_fusion, s32[128]{0:T(128)S(1)} %iota_add_fusion.2, f32[2,128,128]{2,1,0:T(8,128)S(1)} %get-tuple-element.3), kind=kOutput, calls=%fused_computation.181 | convolution fusion | flops 413138944 | bytes 1122820 | tf_op jit(solution)/shard_map/dot_general | solution.py:43
  344.9 6.0 %fusion.102 = f32[2048,128]{1,0:T(8,128)S(1)} fusion(s32[]{:T(128)} %bitcast.7, s32[2048]{0:T(1024)S(1)} %iota_add_fusion, s32[128]{0:T(128)S(1)} %iota_add_fusion.2, f32[2,128,128]{2,1,0:T(8,128)S(1)} %get-tuple-element.3), kind=kOutput, calls=%fused_computation.179 | convolution fusion | flops 413138944 | bytes 1122820 | tf_op jit(solution)/shard_map/dot_general | solution.py:43
  350.9 6.1 %fusion.103 = f32[2048,128]{1,0:T(8,128)S(1)} fusion(s32[]{:T(128)} %bitcast.9, s32[2048]{0:T(1024)S(1)} %iota_add_fusion, s32[128]{0:T(128)S(1)} %iota_add_fusion.2, f32[2,128,128]{2,1,0:T(8,128)S(1)} %get-tuple-element.3), kind=kOutput, calls=%fused_computation.180 | convolution fusion | flops 413138944 | bytes 1122820 | tf_op jit(solution)/shard_map/dot_general | solution.py:43
  357.0 6.0 %fusion.101 = f32[2048,128]{1,0:T(8,128)S(1)} fusion(s32[]{:T(128)} %bitcast.7, s32[2048]{0:T(1024)S(1)} %iota_add_fusion, s32[128]{0:T(128)S(1)} %iota_add_fusion.2, f32[2,128,128]{2,1,0:T(8,128)S(1)} %get-tuple-element.3), kind=kOutput, calls=%fused_computation.178 | convolution fusion | flops 413138944 | bytes 1122820 | tf_op jit(solution)/shard_map/dot_general | solution.py:43
  363.0 7.3 %fusion.20 = bf16[2048,128]{1,0:T(8,128)(2,1)} fusion(f32[2048,128]{1,0:T(8,128)S(1)} %fusion.104, s32[]{:T(128)} %bitcast.9, s32[2048]{0:T(1024)S(1)} %iota_add_fusion, s32[128]{0:T(128)S(1)} %iota_add_fusion.2, f32[2,128,128]{2,1,0:T(8,128)S(1)} %get-tuple-element.2), kind=kOutput, calls=%fused_computation.39 | convolution fusion | flops 413663232 | bytes 1647108 | tf_op jit(solution)/shard_map/dot_general | solution.py:43
  370.3 7.0 %fusion.18 = bf16[2048,128]{1,0:T(8,128)(2,1)} fusion(f32[2048,128]{1,0:T(8,128)S(1)} %fusion.102, s32[]{:T(128)} %bitcast.7, s32[2048]{0:T(1024)S(1)} %iota_add_fusion, s32[128]{0:T(128)S(1)} %iota_add_fusion.2, f32[2,128,128]{2,1,0:T(8,128)S(1)} %get-tuple-element.2), kind=kOutput, calls=%fused_computation.37 | convolution fusion | flops 413663232 | bytes 1647108 | tf_op jit(solution)/shard_map/dot_general | solution.py:43
  377.3 6.9 %fusion.19 = bf16[2048,128]{1,0:T(8,128)(2,1)} fusion(f32[2048,128]{1,0:T(8,128)S(1)} %fusion.103, s32[]{:T(128)} %bitcast.9, s32[2048]{0:T(1024)S(1)} %iota_add_fusion, s32[128]{0:T(128)S(1)} %iota_add_fusion.2, f32[2,128,128]{2,1,0:T(8,128)S(1)} %get-tuple-element.2), kind=kOutput, calls=%fused_computation.38 | convolution fusion | flops 413663232 | bytes 1647108 | tf_op jit(solution)/shard_map/dot_general | solution.py:43
  384.2 7.4 %fusion.17 = bf16[2048,128]{1,0:T(8,128)(2,1)} fusion(f32[2048,128]{1,0:T(8,128)S(1)} %fusion.101, s32[]{:T(128)} %bitcast.7, s32[2048]{0:T(1024)S(1)} %iota_add_fusion, s32[128]{0:T(128)S(1)} %iota_add_fusion.2, f32[2,128,128]{2,1,0:T(8,128)S(1)} %get-tuple-element.2), kind=kOutput, calls=%fused_computation.36 | convolution fusion | flops 413663232 | bytes 1647108 | tf_op jit(solution)/shard_map/dot_general | solution.py:43
  391.6 6.7 %fusion.21 = f32[2048,2048]{1,0:T(8,128)S(1)} fusion(bf16[2048,128]{1,0:T(8,128)(2,1)} %fusion.20, bf16[2048,128]{1,0:T(8,128)(2,1)} %fusion.19, bf16[2048,128]{1,0:T(8,128)(2,1)} %fusion.18, bf16[2048,128]{1,0:T(8,128)(2,1)} %fusion.17, bf16[128,1024]{1,0:T(8,128)(2,1)} %get-tuple-element.6, bf16[128,1024]{1,0:T(8,128)(2,1)} %get-tuple-element.9, ...), kind=kOutput, calls=%fused_computation.40 | convolution fusion | flops 4320133120 | bytes 20447232 | tf_op jit(solution)/shard_map/dot_general | solution.py:115
  398.3 12.8 %fusion = f32[2048,1024]{1,0:T(8,128)} fusion(f32[2048,2048]{1,0:T(8,128)S(1)} %fusion.21, f32[2048,1024]{1,0:T(8,128)S(1)} %bitcast.63, f32[]{:T(128)S(6)} %mul.467, f32[]{:T(128)S(6)} %mul.464, f32[]{:T(128)S(6)} %mul.461, f32[]{:T(128)S(6)} %mul.458, f32[]{:T(128)S(6)} %mul.455, f32[]{:T(128)S(6)} %mul.452, f32[]{:T(128)} %bitcast.11, f32[]{:T(128)S(6)} %mul.380, ...), kind=kLoop, calls=%fused_computation.2 | loop fusion | flops 79691776 | bytes 33554488 | tf_op jit(solution)/shard_map/sub | solution.py:120
  (31 shorter events, 17.6 us)
Async XLA Ops:
  7.2 207.3 %all-reduce.3.cloned.1.call-start = ((), (), s32[]{:S(2)}) async-start(), calls=%async_computation | async-start | bytes 8388608 | tf_op jit(solution)/shard_map/psum | solution.py:83
  14.5 24.1 %slice-start = ((s8[8388608]{0:T(1024)(128)(4,1)}), s8[4194304]{0:T(1024)(128)(4,1)S(1)}, s32[]{:S(2)}) async-start(s8[8388608]{0:T(1024)(128)(4,1)} %bitcast.60), calls=%async_computation.2 | async-start | bytes 8388608
  23.1 15.5 %slice-start.1 = ((s8[8388608]{0:T(1024)(128)(4,1)}), s8[4194304]{0:T(1024)(128)(4,1)S(1)}, s32[]{:S(2)}) async-start(s8[8388608]{0:T(1024)(128)(4,1)} %bitcast.60), calls=%async_computation.3 | async-start | bytes 8388608
  54.2 283.8 %all-reduce.5.cloned.1.call-start = ((), (), s32[]{:S(2)}) async-start(), calls=%async_computation.1 | async-start | bytes 524288 | tf_op jit(solution)/shard_map/psum | solution.py:91
  214.5 7.5 %copy-start.2 = (f32[2048,512]{1,0:T(8,128)S(1)}, f32[2048,512]{1,0:T(8,128)}, u32[]{:S(2)}) copy-start(f32[2048,512]{1,0:T(8,128)} %all-reduce.3.cloned.1.call-done) | copy-start | bytes 12582916
  258.2 79.8 %copy-start.1 = (f32[2,128,128]{2,1,0:T(8,128)S(1)}, f32[2,128,128]{2,1,0:T(8,128)}, u32[]{:S(2)}) copy-start(f32[2,128,128]{2,1,0:T(8,128)} %param.7) | copy-start | bytes 393220
  384.2 14.0 %slice-start.2 = ((s8[8388608]{0:T(1024)(128)(4,1)}), s8[4194304]{0:T(1024)(128)(4,1)S(1)}, s32[]{:S(2)}) async-start(s8[8388608]{0:T(1024)(128)(4,1)} %bitcast.62), calls=%async_computation.4 | async-start | bytes 8388608
  391.6 6.7 %slice-start.3 = ((s8[8388608]{0:T(1024)(128)(4,1)}), s8[4194304]{0:T(1024)(128)(4,1)S(1)}, s32[]{:S(2)}) async-start(s8[8388608]{0:T(1024)(128)(4,1)} %bitcast.62), calls=%async_computation.5 | async-start | bytes 8388608
  398.3 12.8 %copy-start = (f32[2,2,128,128]{3,2,1,0:T(8,128)S(1)}, f32[2,2,128,128]{3,2,1,0:T(8,128)}, u32[]{:S(2)}) copy-start(f32[2,2,128,128]{3,2,1,0:T(8,128)} %all-reduce.5.cloned.1.call-done) | copy-start | bytes 786436
Sparse Core Ops, SparseCore 0:
  54.3 160.1 all-reduce.2
  265.1 72.8 all-reduce.4
where the time goes:
time: 425 us; the launch traced here: 419 us
  waiting for transfers between devices  212 us (50%)
  matrix products  140 us (33%)
  other arithmetic  41.2 us (10%)
  between operations  22.1 us (5%)
    psum x1, waiting for transfers between devices, body(): partial_value = lax.psum(partial_value, 'col')  145 us
    dot_general x16, matrix products, exact(): jnp.dot(left, right, precision=lax.Precision.HIGHEST, preferred_element_t...  102 us
    psum x1, waiting for transfers between devices, body(): field = lax.psum(rows_section(row_tables, part_r, part_i), 'row')  66.3 us
    dot_general x1, matrix products, body(): jnp.dot(imag_b, right_imag, preferred_element_type=jnp.float32)  15.5 us
    dot_general x1, matrix products, body(): jnp.dot(real_b, right_real, preferred_element_type=jnp.float32)  15.5 us
    sub x1, other arithmetic, body(): real_slope * combined[:, :loc_cols] - imag_slope * combined[:, loc_cols:]  12.8 us
  transfers between devices with their start and end apart: 2, of which 2 were waited for; matrix products, arithmetic and copies ran while one was open for 3% of the time, Pallas kernels for 0%

commit v1 on v0

v1 whole, which is shorter than its diff:
```python
import functools
import math

import jax
import jax.numpy as jnp
from jax import lax
from jax.experimental import pallas as pl
from jax.experimental.pallas import tpu as pltpu
from jax.sharding import PartitionSpec as P

MESH = pl.DeviceIdType.MESH
F32, BF16 = jnp.float32, jnp.bfloat16
AXIS = 4
CHIPS = 64
CHUNK = 256


def hops(off):
    return sum(min(a, AXIS - a) for a in off)


OFFSETS = sorted(
    (
        (a, b, c)
        for a in range(AXIS)
        for b in range(AXIS)
        for c in range(AXIS)
        if (a, b, c) != (0, 0, 0)
    ),
    key=lambda off: -hops(off),
)


def coords():
    row, col = lax.axis_index("row"), lax.axis_index("col")
    x, y_lo = row % 4, row // 4
    core, y_hi, z = col % 2, (col // 2) % 2, col // 4
    return x, y_hi * 2 + y_lo, z, core


def device(x, y, z, core):
    return ((y % 2) * 4 + x, (z * 2 + y // 2) * 2 + core)


def monomials(c):
    return [
        c[0] - c[2] + c[4] - c[6],
        c[1] - 3.0 * c[3] + 5.0 * c[5] - 7.0 * c[7],
        2.0 * c[2] - 8.0 * c[4] + 18.0 * c[6],
        4.0 * c[3] - 20.0 * c[5] + 56.0 * c[7],
        8.0 * c[4] - 48.0 * c[6],
        16.0 * c[5] - 112.0 * c[7],
        32.0 * c[6],
        64.0 * c[7],
    ]


def horner(x, coefs):
    acc = coefs[-1] * x + coefs[-2]
    for c in coefs[-3::-1]:
        acc = acc * x + c
    return acc


def chirp_rows(first, width, total, steps):
    shape = (8, width)
    u = lax.broadcasted_iota(jnp.int32, shape, 1) + first
    r = lax.broadcasted_iota(jnp.int32, shape, 0)
    mask = 2 * total - 1
    step = jnp.where((r & 2) == 0, steps[0], steps[1])
    off = u & mask
    k = (((off * off) & mask) * step) & mask
    k = (k - (r & 1) * (total // 2)) & mask
    p = total // 2 - jnp.minimum(k, 2 * total - k)
    a = p.astype(F32) * (math.pi / total)
    s = a * a
    poly = horner(s, [(-1.0) ** n / math.factorial(2 * n + 1) for n in range(7)])
    return a * poly * (1.0 / math.sqrt(total))


def across(seq, r, width):
    x = jnp.broadcast_to(seq[r : r + 1, :], (128, width + 128))
    return pltpu.roll(x, 0, 1, stride=1, stride_axis=0)[:, 128:]


def down(seq, r, block, blocks):
    lo = (blocks - 1 - block) * 128
    x = jnp.broadcast_to(seq[r : r + 1, lo : lo + 256], (128, 256))
    return pltpu.roll(x, 0, 1, stride=1, stride_axis=0)[:, 128:]


def forward_kernel(
    total,
    design_hbm,
    coef,
    steps,
    field_ref,
    dtr_ref,
    dti_ref,
    at_ref,
    wb_ref,
    x_ref,
    t0,
    t1,
    wcol,
    rtab,
    qh,
    ql,
    partial,
    sib,
    pieces,
    landed,
    load_sem,
    sib_send,
    sib_recv,
    rs_send,
    rs_recv,
    ag_send,
    ag_recv,
):
    rows, cols = x_ref.shape
    chunks = rows // CHUNK
    x, y, z, core = coords()
    chip = (x * AXIS + y) * AXIS + z
    other = 1 - core
    sibling = device(x, y, z, other)

    def peer(off):
        px, py, pz = (x + off[0]) % AXIS, (y + off[1]) % AXIS, (z + off[2]) % AXIS
        return (px * AXIS + py) * AXIS + pz, device(px, py, pz, core)

    loads = []
    for i in range(chunks):
        part = pl.ds(i * CHUNK, CHUNK)
        load = pltpu.make_async_copy(design_hbm.at[part], x_ref.at[part], load_sem.at[i])
        load.start()
        loads.append(load)

    barrier = pltpu.get_barrier_semaphore()
    pl.semaphore_signal(barrier, inc=1, device_id=sibling, device_id_type=MESH)
    for off in OFFSETS:
        pl.semaphore_signal(barrier, inc=1, device_id=peer(off)[1], device_id_type=MESH)

    step = [steps[0], steps[1]]
    first_row = lax.axis_index("row") * rows - (total // 2 - 64)
    first_col = lax.axis_index("col") * cols - (total // 2 - 64)
    mono = [monomials([coef[i, k] for k in range(8)]) for i in range(2)]

    seq = chirp_rows(-first_col - cols, cols + 128, total, step)
    for d in range(2):
        for b in range(cols // 128):
            re = down(seq, 2 * d, b, cols // 128).astype(BF16)
            im = down(seq, 2 * d + 1, b, cols // 128).astype(BF16)
            j = b * 128
            wcol[j : j + 128, 256 * d : 256 * d + 128] = re
            wcol[j : j + 128, 256 * d + 128 : 256 * d + 256] = im
            wcol[cols + j : cols + j + 128, 256 * d : 256 * d + 128] = -im
            wcol[cols + j : cols + j + 128, 256 * d + 128 : 256 * d + 256] = re
    seq = chirp_rows(first_row - 128, rows + 128, total, step)
    for r in range(4):
        rtab[128 * r : 128 * r + 128, :] = across(seq, r, rows).astype(BF16)

    def transmit(i, t):
        loads[i].wait()
        v = x_ref[i * CHUNK : (i + 1) * CHUNK, :]
        t[:, :cols] = horner(v, mono[0]).astype(BF16)
        t[:, cols:] = horner(v, mono[1]).astype(BF16)

    def contract(i, t):
        q = jnp.dot(t[...], wcol[...], preferred_element_type=F32)
        hi = q.astype(BF16)
        qh[i * CHUNK : (i + 1) * CHUNK, :] = hi
        ql[i * CHUNK : (i + 1) * CHUNK, :] = (q - hi.astype(F32)).astype(BF16)

    slots = [t0, t1]
    transmit(0, t0)
    for i in range(chunks):
        if i + 1 < chunks:
            transmit(i + 1, slots[(i + 1) % 2])
        contract(i, slots[i % 2])

    def focus(d):
        a = rtab[pl.ds(d * 256, 256), :]
        lanes = pl.ds(d * 256, 256)
        f = jnp.dot(a, qh[:, lanes], preferred_element_type=F32) + jnp.dot(
            a, ql[:, lanes], preferred_element_type=F32
        )
        return jnp.concatenate(
            [f[:128, :128] - f[128:, 128:], f[:128, 128:] + f[128:, :128]], axis=0
        )

    partial[...] = focus(other)
    pl.semaphore_wait(barrier, CHIPS)
    give = pltpu.make_async_remote_copy(
        src_ref=partial,
        dst_ref=sib,
        send_sem=sib_send.at[0],
        recv_sem=sib_recv.at[0],
        device_id=sibling,
        device_id_type=MESH,
    )
    give.start()
    own = focus(core)
    give.wait_recv()
    total_chip = own + sib[...]
    for p in range(CHIPS):
        pieces[p] = total_chip[4 * p : 4 * p + 4, :]

    sends = []
    for n, off in enumerate(OFFSETS):
        there, dev = peer(off)
        copy = pltpu.make_async_remote_copy(
            src_ref=pieces.at[there],
            dst_ref=landed.at[n],
            send_sem=rs_send,
            recv_sem=rs_recv,
            device_id=dev,
            device_id_type=MESH,
        )
        copy.start()
        sends.append(copy)

    slopes = [[k * m[k] for k in range(1, 8)] for m in mono]

    @pl.loop(0, rows // 64)
    def _(i):
        part = pl.ds(pl.multiple_of(i * 64, 64), 64)
        v = x_ref[part]
        dtr_ref[part] = horner(v, slopes[0])
        dti_ref[part] = horner(v, slopes[1])

    everything = pl.ds(0, CHIPS - 1)
    pltpu.make_async_copy(landed.at[everything], landed.at[everything], rs_recv).wait()
    total_piece = pieces[chip]
    for n in range(CHIPS - 1):
        total_piece = total_piece + landed[n]
    mine = field_ref.at[core]
    mine[chip] = total_piece
    for n, off in enumerate(OFFSETS):
        dev = peer(off)[1]
        copy = pltpu.make_async_remote_copy(
            src_ref=mine.at[chip],
            dst_ref=mine.at[chip],
            send_sem=ag_send,
            recv_sem=ag_recv,
            device_id=dev,
            device_id_type=MESH,
        )
        copy.start()

    seq = chirp_rows(-first_row - rows, rows + 128, total, step)
    for r in range(4):
        for b in range(rows // 128):
            at_ref[128 * b : 128 * b + 128, 128 * r : 128 * r + 128] = down(
                seq, r, b, rows // 128
            ).astype(BF16)
    seq = chirp_rows(first_col - 128, cols + 128, total, step)
    for d in range(2):
        re = across(seq, 2 * d, cols).astype(BF16)
        im = across(seq, 2 * d + 1, cols).astype(BF16)
        wb_ref[256 * d : 256 * d + 128, :cols] = re
        wb_ref[256 * d : 256 * d + 128, cols:] = im
        wb_ref[256 * d + 128 : 256 * d + 256, :cols] = -im
        wb_ref[256 * d + 128 : 256 * d + 256, cols:] = re

    pltpu.make_async_copy(mine.at[everything], mine.at[everything], ag_recv).wait()
    show = pltpu.make_async_remote_copy(
        src_ref=mine,
        dst_ref=field_ref.at[core],
        send_sem=sib_send.at[1],
        recv_sem=sib_recv.at[1],
        device_id=sibling,
        device_id_type=MESH,
    )
    show.start()
    show.wait_recv()
    give.wait_send()
    pltpu.make_async_copy(landed.at[everything], landed.at[everything], rs_send).wait()
    pltpu.make_async_copy(landed.at[everything], landed.at[everything], ag_send).wait()
    show.wait_send()


def backward_kernel(factor, field_in, target, at, wb, dtr, dti, grad_ref, field_out, v_ref):
    cols = grad_ref.shape[1]
    i = pl.program_id(0)

    @pl.when(i == 0)
    def _():
        for d in range(2):
            for p in range(CHIPS):
                lo = 4 * p
                field_out[d, lo // 128, lo % 128 : lo % 128 + 4, :] = field_in[d, p]
            fr, fi = field_out[d, 0], field_out[d, 1]
            excess = 4.0 * factor * (fr * fr + fi * fi - target[d])
            gr, gi = excess * fr, excess * fi
            g = jnp.concatenate(
                [jnp.concatenate([gr, -gi], axis=1), jnp.concatenate([gi, gr], axis=1)], axis=0
            )
            hi = g.astype(BF16)
            lo = (g - hi.astype(F32)).astype(BF16)
            a = at[:, 256 * d : 256 * d + 256]
            v = jnp.dot(a, hi, preferred_element_type=F32) + jnp.dot(
                a, lo, preferred_element_type=F32
            )
            v_ref[:, 256 * d : 256 * d + 256] = v.astype(BF16)

    rows = grad_ref.shape[0]
    part = pl.ds(pl.multiple_of(i * rows, rows), rows)
    v = v_ref[part, :]
    wide = 256
    for n in range(cols // wide):
        lanes = slice(n * wide, (n + 1) * wide)
        hr = jnp.dot(v, wb[:, lanes], preferred_element_type=F32)
        hi = jnp.dot(
            v, wb[:, cols + n * wide : cols + (n + 1) * wide], preferred_element_type=F32
        )
        grad_ref[:, lanes] = dtr[part, lanes] * hr - dti[part, lanes] * hi


def body(design, coefficients, focal_steps, target):
    rows, cols = design.shape
    total = rows * lax.axis_size("row")
    focal = target.shape[1]
    vmem = pl.BlockSpec(memory_space=pltpu.VMEM)
    smem = pl.BlockSpec(memory_space=pltpu.SMEM)
    dma = pltpu.SemaphoreType.DMA
    field, dtr, dti, at, wb = pl.pallas_call(
        functools.partial(forward_kernel, total),
        out_shape=(
            pltpu.VMEM((2, CHIPS, 4, 128), F32),
            pltpu.VMEM((rows, cols), F32),
            pltpu.VMEM((rows, cols), F32),
            pltpu.VMEM((rows, 512), BF16),
            pltpu.VMEM((512, 2 * cols), BF16),
        ),
        in_specs=[pl.BlockSpec(memory_space=pl.ANY), smem, smem],
        out_specs=(vmem,) * 5,
        scratch_shapes=[
            pltpu.VMEM((rows, cols), F32),
            pltpu.VMEM((CHUNK, 2 * cols), BF16),
            pltpu.VMEM((CHUNK, 2 * cols), BF16),
            pltpu.VMEM((2 * cols, 512), BF16),
            pltpu.VMEM((512, rows), BF16),
            pltpu.VMEM((rows, 512), BF16),
            pltpu.VMEM((rows, 512), BF16),
            pltpu.VMEM((256, 128), F32),
            pltpu.VMEM((256, 128), F32),
            pltpu.VMEM((CHIPS, 4, 128), F32),
            pltpu.VMEM((CHIPS, 4, 128), F32),
            dma((rows // CHUNK,)),
            dma((2,)),
            dma((2,)),
            dma,
            dma,
            dma,
            dma,
        ],
        compiler_params=pltpu.CompilerParams(
            collective_id=0, has_side_effects=True, vmem_limit_bytes=36 * 2**20
        ),
        name="forward",
    )(design, coefficients, focal_steps)

    factor = math.sqrt(total * total) / (4.0 * focal)
    step_rows = 256
    gradient, field = pl.pallas_call(
        functools.partial(backward_kernel, factor),
        grid=(rows // step_rows,),
        out_shape=(
            jax.ShapeDtypeStruct((rows, cols), F32),
            jax.ShapeDtypeStruct((2, 2, focal, focal), F32),
        ),
        in_specs=[vmem] * 6,
        out_specs=(
            pl.BlockSpec((step_rows, cols), lambda i: (i, 0)),
            pl.BlockSpec((2, 2, focal, focal), lambda i: (0, 0, 0, 0)),
        ),
        scratch_shapes=[pltpu.VMEM((rows, 512), BF16)],
        compiler_params=pltpu.CompilerParams(vmem_limit_bytes=20 * 2**20),
        name="backward",
    )(field, target, at, wb, dtr, dti)
    return gradient, field


def solution(mesh):
    return jax.shard_map(
        body,
        mesh=mesh,
        in_specs=(P("row", "col"), P(), P(), P()),
        out_specs=(P("row", "col"), P()),
        check_vma=False,
    )
```

time: 425 us -> 63.7 us (0.15)
  the two profiles are of different devices: /device:TPU:0 before, /device:TPU:1 now
where the time goes in v1:
time: 63.7 us; the launch traced here: 63.5 us
  Pallas kernels  56.1 us (88%)
  local copies, waits for them, and re-layouts  6.78 us (11%)
  between operations  0.66 us (1%)
    pallas_call x1, Pallas kernels, body(): pl.pallas_call(functools.partial(forward_kernel, total), out_shape=(pltpu...  47.1 us
    pallas_call x1, Pallas kernels, body(): pl.pallas_call(functools.partial(backward_kernel, factor), grid=(rows //...  9 us
    unnamed x6, local copies, waits for them, and re-layouts  6.78 us

profile of v1, /device:TPU:1, one launch (start us, length us, event | category | flops | bytes accessed | tf_op | source)
XLA Modules:
  0.0 63.5 jit_solution(10534397549011187768)
XLA Ops:
  0.6 0.0 copy-start.2
  0.6 47.1 %forward.1 = (f32[2,64,4,128]{3,2,1,0:T(4,128)S(1)}, f32[2048,1024]{1,0:T(8,128)S(1)}, f32[2048,1024]{1,0:T(8,128)S(1)}, bf16[2048,512]{1,0:T(8,128)(2,1)S(1)}, bf16[512,2048]{1,0:T(8,128)(2,1)S(1)}) custom-call(f32[2048,1024]{1,0:T(8,128)} %design_hbm.1, f32[2,8]{1,0:T(2,128)} %coef.1, s32[2]{0:T(128)} %steps.1), custom_call_target="tpu_custom_call" | custom-call | tf_op jit(solution)/shard_map/forward/pallas_call | solution.py:327
  47.7 0.0 copy-start
  47.7 3.4 %copy-done = f32[2048,1024]{1,0:T(8,128)} copy-done((f32[2048,1024]{1,0:T(8,128)}, f32[2048,1024]{1,0:T(8,128)S(1)}, u32[]{:S(2)}) %copy-start) | copy-done | bytes 8388632
  51.1 0.0 copy-done.2
  51.1 0.0 copy-start.1
  51.1 3.4 %copy-done.1 = f32[2048,1024]{1,0:T(8,128)S(1)} copy-done((f32[2048,1024]{1,0:T(8,128)S(1)}, f32[2048,1024]{1,0:T(8,128)}, u32[]{:S(2)}) %copy-start.1) | copy-done | bytes 8388632
  54.5 9.0 %backward.1 = (f32[2048,1024]{1,0:T(8,128)}, f32[2,2,128,128]{3,2,1,0:T(8,128)}) custom-call(f32[2,64,4,128]{3,2,1,0:T(4,128)S(1)} %get-tuple-element.7.field_in, f32[2,128,128]{2,1,0:T(8,128)S(1)} %copy-done.2, bf16[2048,512]{1,0:T(8,128)(2,1)S(1)} %get-tuple-element.8.at, bf16[512,2048]{1,0:T(8,128)(2,1)S(1)} %get-tuple-element.9.wb, ...), custom_call_target="tpu_custom_call" | custom-call | tf_op jit(solution)/shard_map/backward/pallas_call | solution.py:366
Async XLA Ops:
  0.6 50.5 %copy-start.2 = (f32[2,128,128]{2,1,0:T(8,128)S(1)}, f32[2,128,128]{2,1,0:T(8,128)}, u32[]{:S(2)}) copy-start(f32[2,128,128]{2,1,0:T(8,128)} %target.1) | copy-start | bytes 393220
  47.7 3.4 %copy-start = (f32[2048,1024]{1,0:T(8,128)}, f32[2048,1024]{1,0:T(8,128)S(1)}, u32[]{:S(2)}) copy-start(f32[2048,1024]{1,0:T(8,128)S(1)} %get-tuple-element.10.dtr) | copy-start | bytes 25165828
  51.1 3.4 %copy-start.1 = (f32[2048,1024]{1,0:T(8,128)S(1)}, f32[2048,1024]{1,0:T(8,128)}, u32[]{:S(2)}) copy-start(f32[2048,1024]{1,0:T(8,128)} %copy-done) | copy-start | bytes 25165828

commit v2 on v1

v2 whole, which is shorter than its diff:
```python
import functools
import math

import jax
import jax.numpy as jnp
from jax import lax
from jax.experimental import pallas as pl
from jax.experimental.pallas import tpu as pltpu
from jax.sharding import PartitionSpec as P

MESH = pl.DeviceIdType.MESH
F32, BF16 = jnp.float32, jnp.bfloat16
AXIS = 4
CHIPS = 64
CHUNK = 256
MROWS = 512


def hops(off):
    return sum(min(a, AXIS - a) for a in off)


OFFSETS = sorted(
    (
        (a, b, c)
        for a in range(AXIS)
        for b in range(AXIS)
        for c in range(AXIS)
        if (a, b, c) != (0, 0, 0)
    ),
    key=lambda off: -hops(off),
)


def coords():
    row, col = lax.axis_index("row"), lax.axis_index("col")
    x, y_lo = lax.rem(row, 4), lax.div(row, 4)
    core, y_hi, z = lax.rem(col, 2), lax.rem(lax.div(col, 2), 2), lax.div(col, 4)
    return x, y_hi * 2 + y_lo, z, core


def device(x, y, z, core):
    return (lax.rem(y, 2) * 4 + x, (z * 2 + lax.div(y, 2)) * 2 + core)


def monomials(c):
    return [
        c[0] - c[2] + c[4] - c[6],
        c[1] - 3.0 * c[3] + 5.0 * c[5] - 7.0 * c[7],
        2.0 * c[2] - 8.0 * c[4] + 18.0 * c[6],
        4.0 * c[3] - 20.0 * c[5] + 56.0 * c[7],
        8.0 * c[4] - 48.0 * c[6],
        16.0 * c[5] - 112.0 * c[7],
        32.0 * c[6],
        64.0 * c[7],
    ]


def horner(x, coefs):
    acc = coefs[-1] * x + coefs[-2]
    for c in coefs[-3::-1]:
        acc = acc * x + c
    return acc


def chirp_rows(first, width, total, steps):
    shape = (8, width)
    u = lax.broadcasted_iota(jnp.int32, shape, 1) + first
    r = lax.broadcasted_iota(jnp.int32, shape, 0)
    mask = 2 * total - 1
    step = jnp.where((r & 2) == 0, steps[0], steps[1])
    off = u & mask
    k = (((off * off) & mask) * step) & mask
    k = (k - (r & 1) * (total // 2)) & mask
    p = total // 2 - jnp.minimum(k, 2 * total - k)
    a = p.astype(F32) * (math.pi / total)
    s = a * a
    poly = horner(s, [(-1.0) ** n / math.factorial(2 * n + 1) for n in range(7)])
    return a * poly * (1.0 / math.sqrt(total))


def across(seq, r, width):
    x = jnp.broadcast_to(seq[pl.ds(r, 1), : width + 128], (128, width + 128))
    return pltpu.roll(x, 0, 1, stride=1, stride_axis=0)[:, 128:].astype(BF16)


def down(seq, r, lo):
    x = jnp.broadcast_to(seq[r : r + 1, pl.ds(pl.multiple_of(lo, 128), 256)], (128, 256))
    return pltpu.roll(x, 0, 1, stride=1, stride_axis=0)[:, 128:].astype(BF16)


def forward_kernel(
    total,
    design_hbm,
    coef,
    steps,
    target_hbm,
    field_ref,
    dtr_ref,
    dti_ref,
    at_ref,
    wb_ref,
    target_ref,
    x_ref,
    t_ref,
    wcol,
    rtab,
    qh,
    ql,
    seq,
    partial,
    sib,
    pieces,
    landed,
    load_sem,
    sib_send,
    sib_recv,
    rs_send,
    rs_recv,
    ag_send,
    ag_recv,
):
    rows, cols = x_ref.shape
    chunks = rows // CHUNK
    x, y, z, core = coords()
    chip = (x * AXIS + y) * AXIS + z
    other = 1 - core
    sibling = device(x, y, z, other)

    def load(i):
        part = pl.ds(pl.multiple_of(i * CHUNK, CHUNK), CHUNK)
        return pltpu.make_async_copy(design_hbm.at[part], x_ref.at[part], load_sem.at[i])

    for i in range(chunks):
        load(i).start()
    fetch = pltpu.make_async_copy(target_hbm, target_ref, load_sem.at[chunks])
    fetch.start()

    xs = [lax.rem(x + a, AXIS) for a in range(AXIS)]
    ys = [lax.rem(y + a, AXIS) for a in range(AXIS)]
    zs = [lax.rem(z + a, AXIS) for a in range(AXIS)]
    y_row = [lax.rem(a, 2) * AXIS for a in ys]
    y_col = [lax.div(a, 2) * 2 + core for a in ys]
    peers = [
        (
            xs[a] * (AXIS * AXIS) + ys[b] * AXIS + zs[c],
            (y_row[b] + xs[a], zs[c] * AXIS + y_col[b]),
        )
        for a, b, c in OFFSETS
    ]

    barrier = pltpu.get_barrier_semaphore()
    pl.semaphore_signal(barrier, inc=1, device_id=sibling, device_id_type=MESH)

    for _, dev in peers:
        pl.semaphore_signal(barrier, inc=1, device_id=dev, device_id_type=MESH)

    step = [steps[0], steps[1]]
    first_row = lax.axis_index("row") * rows - (total // 2 - 64)
    first_col = lax.axis_index("col") * cols - (total // 2 - 64)
    mono = [monomials([coef[i, k] for k in range(8)]) for i in range(2)]

    seq[:, : cols + 128] = chirp_rows(-first_col - cols, cols + 128, total, step)

    @pl.loop(0, cols // 128)
    def _(b):
        upper = pl.ds(pl.multiple_of(b * 128, 128), 128)
        lower = pl.ds(pl.multiple_of(cols + b * 128, 128), 128)
        lo = cols - 128 - b * 128
        for d in range(2):
            re, im = down(seq, 2 * d, lo), down(seq, 2 * d + 1, lo)
            wcol[upper, 256 * d : 256 * d + 128] = re
            wcol[upper, 256 * d + 128 : 256 * d + 256] = im
            wcol[lower, 256 * d : 256 * d + 128] = -im
            wcol[lower, 256 * d + 128 : 256 * d + 256] = re

    seq[...] = chirp_rows(first_row - 128, rows + 128, total, step)

    @pl.loop(0, 4)
    def _(r):
        rtab[pl.ds(pl.multiple_of(128 * r, 128), 128), :] = across(seq, r, rows)

    @pl.loop(0, chunks)
    def _(i):
        load(i).wait()

        @pl.loop(0, CHUNK // 32)
        def _(j):
            part = pl.ds(pl.multiple_of(i * CHUNK + j * 32, 32), 32)
            v = x_ref[part]
            t_ref[part, :cols] = horner(v, mono[0]).astype(BF16)
            t_ref[part, cols:] = horner(v, mono[1]).astype(BF16)

    @pl.loop(0, rows // MROWS)
    def _(i):
        part = pl.ds(pl.multiple_of(i * MROWS, MROWS), MROWS)
        q = jnp.dot(t_ref[part], wcol[...], preferred_element_type=F32)
        hi = q.astype(BF16)
        qh[part] = hi
        ql[part] = (q - hi.astype(F32)).astype(BF16)

    pl.semaphore_wait(barrier, CHIPS)
    give = pltpu.make_async_remote_copy(
        src_ref=partial.at[0],
        dst_ref=sib,
        send_sem=sib_send.at[0],
        recv_sem=sib_recv.at[0],
        device_id=sibling,
        device_id_type=MESH,
    )

    @pl.loop(0, 2)
    def _(i):
        d = other + i * (2 * core - 1)
        a = rtab[pl.ds(pl.multiple_of(d * 256, 256), 256), :]
        lanes = pl.ds(pl.multiple_of(d * 256, 256), 256)
        f = jnp.dot(a, qh[:, lanes], preferred_element_type=F32) + jnp.dot(
            a, ql[:, lanes], preferred_element_type=F32
        )
        partial[i, :128] = f[:128, :128] - f[128:, 128:]
        partial[i, 128:] = f[:128, 128:] + f[128:, :128]

        @pl.when(i == 0)
        def _():
            give.start()

    fetch.wait()
    give.wait_recv()
    total_chip = partial[1] + sib[...]
    for p in range(CHIPS):
        pieces[p] = total_chip[4 * p : 4 * p + 4, :]

    for n, (there, dev) in enumerate(peers):
        pltpu.make_async_remote_copy(
            src_ref=pieces.at[there],
            dst_ref=landed.at[n],
            send_sem=rs_send,
            recv_sem=rs_recv,
            device_id=dev,
            device_id_type=MESH,
        ).start()

    slopes = [[k * m[k] for k in range(1, 8)] for m in mono]

    @pl.loop(0, rows // 32)
    def _(i):
        part = pl.ds(pl.multiple_of(i * 32, 32), 32)
        v = x_ref[part]
        dtr_ref[part] = horner(v, slopes[0])
        dti_ref[part] = horner(v, slopes[1])

    everything = pl.ds(0, CHIPS - 1)
    pltpu.make_async_copy(landed.at[everything], landed.at[everything], rs_recv).wait()
    total_piece = pieces[chip]
    for n in range(CHIPS - 1):
        total_piece = total_piece + landed[n]
    mine = field_ref.at[core]
    mine[chip] = total_piece

    for _, dev in peers:
        pltpu.make_async_remote_copy(
            src_ref=mine.at[chip],
            dst_ref=mine.at[chip],
            send_sem=ag_send,
            recv_sem=ag_recv,
            device_id=dev,
            device_id_type=MESH,
        ).start()

    seq[...] = chirp_rows(-first_row - rows, rows + 128, total, step)

    @pl.loop(0, rows // 128)
    def _(b):
        part = pl.ds(pl.multiple_of(b * 128, 128), 128)
        for r in range(4):
            at_ref[part, 128 * r : 128 * r + 128] = down(seq, r, rows - 128 - b * 128)

    seq[:, : cols + 128] = chirp_rows(first_col - 128, cols + 128, total, step)

    @pl.loop(0, 2)
    def _(d):
        re, im = across(seq, 2 * d, cols), across(seq, 2 * d + 1, cols)
        upper = pl.ds(pl.multiple_of(256 * d, 128), 128)
        lower = pl.ds(pl.multiple_of(256 * d + 128, 128), 128)
        wb_ref[upper, :cols] = re
        wb_ref[upper, cols:] = im
        wb_ref[lower, :cols] = -im
        wb_ref[lower, cols:] = re

    pltpu.make_async_copy(mine.at[everything], mine.at[everything], ag_recv).wait()
    show = pltpu.make_async_remote_copy(
        src_ref=mine,
        dst_ref=field_ref.at[core],
        send_sem=sib_send.at[1],
        recv_sem=sib_recv.at[1],
        device_id=sibling,
        device_id_type=MESH,
    )
    show.start()
    show.wait_recv()
    give.wait_send()
    pltpu.make_async_copy(landed.at[everything], landed.at[everything], rs_send).wait()
    pltpu.make_async_copy(landed.at[everything], landed.at[everything], ag_send).wait()
    show.wait_send()


def backward_kernel(factor, field_in, target, at, wb, dtr, dti, grad_ref, field_out, v_ref, g_ref):
    rows, cols = dtr.shape
    i = pl.program_id(0)

    @pl.when(i == 0)
    def _():
        for d in range(2):
            for p in range(CHIPS):
                lo = 4 * p
                field_out[d, lo // 128, lo % 128 : lo % 128 + 4, :] = field_in[d, p]
            fr, fi = field_out[d, 0], field_out[d, 1]
            excess = 4.0 * factor * (fr * fr + fi * fi - target[d])
            gr, gi = excess * fr, excess * fi
            g_ref[d] = jnp.concatenate(
                [jnp.concatenate([gr, -gi], axis=1), jnp.concatenate([gi, gr], axis=1)], axis=0
            ).astype(BF16)

        @pl.loop(0, rows // MROWS)
        def _(j):
            part = pl.ds(pl.multiple_of(j * MROWS, MROWS), MROWS)
            for d in range(2):
                v = jnp.dot(
                    at[part, 256 * d : 256 * d + 256], g_ref[d], preferred_element_type=F32
                )
                v_ref[part, 256 * d : 256 * d + 256] = v.astype(BF16)

    height = grad_ref.shape[0]
    part = pl.ds(pl.multiple_of(i * height, height), height)
    v = v_ref[part, :]
    for n in range(cols // 256):
        left = slice(n * 256, (n + 1) * 256)
        right = slice(cols + n * 256, cols + (n + 1) * 256)
        hr = jnp.dot(v, wb[:, left], preferred_element_type=F32)
        hi = jnp.dot(v, wb[:, right], preferred_element_type=F32)
        grad_ref[:, left] = dtr[part, left] * hr - dti[part, left] * hi


def body(design, coefficients, focal_steps, target):
    rows, cols = design.shape
    total = rows * lax.axis_size("row")
    focal = target.shape[1]
    vmem = pl.BlockSpec(memory_space=pltpu.VMEM)
    smem = pl.BlockSpec(memory_space=pltpu.SMEM)
    dma = pltpu.SemaphoreType.DMA
    field, dtr, dti, at, wb, target = pl.pallas_call(
        functools.partial(forward_kernel, total),
        out_shape=(
            pltpu.VMEM((2, CHIPS, 4, 128), F32),
            pltpu.VMEM((rows, cols), F32),
            pltpu.VMEM((rows, cols), F32),
            pltpu.VMEM((rows, 512), BF16),
            pltpu.VMEM((512, 2 * cols), BF16),
            pltpu.VMEM(target.shape, F32),
        ),
        in_specs=[pl.BlockSpec(memory_space=pl.ANY), smem, smem, pl.BlockSpec(memory_space=pl.ANY)],
        out_specs=(vmem,) * 6,
        scratch_shapes=[
            pltpu.VMEM((rows, cols), F32),
            pltpu.VMEM((rows, 2 * cols), BF16),
            pltpu.VMEM((2 * cols, 512), BF16),
            pltpu.VMEM((512, rows), BF16),
            pltpu.VMEM((rows, 512), BF16),
            pltpu.VMEM((rows, 512), BF16),
            pltpu.VMEM((8, rows + 128), F32),
            pltpu.VMEM((2, 256, 128), F32),
            pltpu.VMEM((256, 128), F32),
            pltpu.VMEM((CHIPS, 4, 128), F32),
            pltpu.VMEM((CHIPS, 4, 128), F32),
            dma((rows // CHUNK + 1,)),
            dma((2,)),
            dma((2,)),
            dma,
            dma,
            dma,
            dma,
        ],
        compiler_params=pltpu.CompilerParams(
            collective_id=0, has_side_effects=True, vmem_limit_bytes=30 * 2**20
        ),
        name="forward",
    )(design, coefficients, focal_steps, target)

    factor = math.sqrt(total * total) / (4.0 * focal)
    height = MROWS
    gradient, field = pl.pallas_call(
        functools.partial(backward_kernel, factor),
        grid=(rows // height,),
        out_shape=(
            jax.ShapeDtypeStruct((rows, cols), F32),
            jax.ShapeDtypeStruct((2, 2, focal, focal), F32),
        ),
        in_specs=[vmem] * 6,
        out_specs=(
            pl.BlockSpec((height, cols), lambda i: (i, 0)),
            pl.BlockSpec((2, 2, focal, focal), lambda i: (0, 0, 0, 0)),
        ),
        scratch_shapes=[pltpu.VMEM((rows, 512), BF16), pltpu.VMEM((2, 256, 256), BF16)],
        compiler_params=pltpu.CompilerParams(vmem_limit_bytes=14 * 2**20),
        name="backward",
    )(field, target, at, wb, dtr, dti)
    return gradient, field


def solution(mesh):
    return jax.shard_map(
        body,
        mesh=mesh,
        in_specs=(P("row", "col"), P(), P(), P()),
        out_specs=(P("row", "col"), P()),
        check_vma=False,
    )
```

time: 63.7 us -> 50.6 us (0.79)
  Pallas kernels: 56.1 us -> 47.5 us
  local copies, waits for them, and re-layouts: 6.78 us -> 2.23 us
    pallas_call x1, Pallas kernels: 47.1 us -> 39.8 us  [body(): pl.pallas_call(functools.partial(forward_kernel, total), out_shape=(pltpu...]
    unnamed x6, local copies, waits for them, and re-layouts: 6.78 us -> 2.23 us
    pallas_call x1, Pallas kernels: 9 us -> 7.76 us  [body(): pl.pallas_call(functools.partial(backward_kernel, factor), grid=(rows //...]
where the time goes in v2:
time: 50.6 us; the launch traced here: 50.4 us
  Pallas kernels  47.5 us (94%)
  local copies, waits for them, and re-layouts  2.23 us (4%)
  between operations  0.65 us (1%)
    pallas_call x1, Pallas kernels, body(): pl.pallas_call(functools.partial(forward_kernel, total), out_shape=(pltpu...  39.8 us
    pallas_call x1, Pallas kernels, body(): pl.pallas_call(functools.partial(backward_kernel, factor), grid=(rows //...  7.76 us
    unnamed x6, local copies, waits for them, and re-layouts  2.23 us

profile of v2, /device:TPU:1, one launch (start us, length us, event | category | flops | bytes accessed | tf_op | source)
XLA Modules:
  0.0 50.4 jit_solution(1260372119842348730)
XLA Ops:
  0.6 0.0 copy-start
  0.6 0.9 %copy-done = f32[2,128,128]{2,1,0:T(8,128)S(1)} copy-done((f32[2,128,128]{2,1,0:T(8,128)S(1)}, f32[2,128,128]{2,1,0:T(8,128)}, u32[]{:S(2)}) %copy-start) | copy-done | bytes 131096
  1.5 0.0 copy-start.1
  1.5 0.7 %copy-done.1 = f32[2,8]{1,0:T(2,128)S(1)} copy-done((f32[2,8]{1,0:T(2,128)S(1)}, f32[2,8]{1,0:T(2,128)}, u32[]{:S(2)}) %copy-start.1) | copy-done | bytes 88
  2.2 0.0 copy-start.2
  2.2 0.7 %copy-done.2 = s32[2]{0:T(128)S(1)} copy-done((s32[2]{0:T(128)S(1)}, s32[2]{0:T(128)}, u32[]{:S(2)}) %copy-start.2) | copy-done | bytes 32
  2.9 39.8 %forward.1 = (f32[2,64,4,128]{3,2,1,0:T(4,128)S(1)}, f32[2048,1024]{1,0:T(8,128)S(1)}, f32[2048,1024]{1,0:T(8,128)S(1)}, bf16[2048,512]{1,0:T(8,128)(2,1)S(1)}, ...) custom-call(f32[2048,1024]{1,0:T(8,128)} %design_hbm.1, f32[2,8]{1,0:T(2,128)S(1)} %copy-done.1, ...), custom_call_target="tpu_custom_call" | custom-call | tf_op jit(solution)/shard_map/forward/pallas_call | solution.py:351
  42.7 7.8 %backward.1 = (f32[2048,1024]{1,0:T(8,128)}, f32[2,2,128,128]{3,2,1,0:T(8,128)}) custom-call(f32[2,64,4,128]{3,2,1,0:T(4,128)S(1)} %get-tuple-element.8.field_in, f32[2,128,128]{2,1,0:T(8,128)S(1)} %get-tuple-element.9.target, bf16[2048,512]{1,0:T(8,128)(2,1)S(1)} %get-tuple-element.10.at, bf16[512,2048]{1,0:T(8,128)(2,1)S(1)} %get-tuple-element.11.wb, ...), custom_call_target="tpu_custom_call" | custom-call | tf_op jit(solution)/shard_map/backward/pallas_call | solution.py:391
Async XLA Ops:
  0.6 0.9 %copy-start = (f32[2,128,128]{2,1,0:T(8,128)S(1)}, f32[2,128,128]{2,1,0:T(8,128)}, u32[]{:S(2)}) copy-start(f32[2,128,128]{2,1,0:T(8,128)} %target_hbm.1) | copy-start | bytes 393220
  1.5 0.7 %copy-start.1 = (f32[2,8]{1,0:T(2,128)S(1)}, f32[2,8]{1,0:T(2,128)}, u32[]{:S(2)}) copy-start(f32[2,8]{1,0:T(2,128)} %coef.1) | copy-start | bytes 196
  2.2 0.7 %copy-start.2 = (s32[2]{0:T(128)S(1)}, s32[2]{0:T(128)}, u32[]{:S(2)}) copy-start(s32[2]{0:T(128)} %steps.1) | copy-start | bytes 28

commit v3 on v2

--- a/solution.py
+++ b/solution.py
@@ -92,8 +92,8 @@
 def forward_kernel(
     total,
     design_hbm,
-    coef,
-    steps,
+    coef_hbm,
+    steps_hbm,
     target_hbm,
     field_ref,
     dtr_ref,
@@ -101,8 +101,11 @@
     at_ref,
     wb_ref,
     target_ref,
+    coef,
+    steps,
     x_ref,
-    t_ref,
+    t0,
+    t1,
     wcol,
     rtab,
     qh,
@@ -131,6 +134,12 @@
         part = pl.ds(pl.multiple_of(i * CHUNK, CHUNK), CHUNK)
         return pltpu.make_async_copy(design_hbm.at[part], x_ref.at[part], load_sem.at[i])
 
+    fetches = [
+        pltpu.make_async_copy(src, dst, load_sem.at[chunks + 1 + n])
+        for n, (src, dst) in enumerate([(steps_hbm, steps), (coef_hbm, coef)])
+    ]
+    for fetch in fetches:
+        fetch.start()
     for i in range(chunks):
         load(i).start()
     fetch = pltpu.make_async_copy(target_hbm, target_ref, load_sem.at[chunks])
@@ -155,6 +164,8 @@
     for _, dev in peers:
         pl.semaphore_signal(barrier, inc=1, device_id=dev, device_id_type=MESH)
 
+    for ready in fetches:
+        ready.wait()
     step = [steps[0], steps[1]]
     first_row = lax.axis_index("row") * rows - (total // 2 - 64)
     first_col = lax.axis_index("col") * cols - (total // 2 - 64)
@@ -180,24 +191,33 @@
     def _(r):
         rtab[pl.ds(pl.multiple_of(128 * r, 128), 128), :] = across(seq, r, rows)
 
-    @pl.loop(0, chunks)
-    def _(i):
-        load(i).wait()
-
-        @pl.loop(0, CHUNK // 32)
-        def _(j):
-            part = pl.ds(pl.multiple_of(i * CHUNK + j * 32, 32), 32)
-            v = x_ref[part]
-            t_ref[part, :cols] = horner(v, mono[0]).astype(BF16)
-            t_ref[part, cols:] = horner(v, mono[1]).astype(BF16)
-
-    @pl.loop(0, rows // MROWS)
-    def _(i):
-        part = pl.ds(pl.multiple_of(i * MROWS, MROWS), MROWS)
-        q = jnp.dot(t_ref[part], wcol[...], preferred_element_type=F32)
+    def transmit(i, t):
+        v = x_ref[pl.ds(pl.multiple_of(i * CHUNK, CHUNK), CHUNK)]
+        t[:, :cols] = horner(v, mono[0]).astype(BF16)
+        t[:, cols:] = horner(v, mono[1]).astype(BF16)
+
+    def contract(i, t):
+        part = pl.ds(pl.multiple_of(i * CHUNK, CHUNK), CHUNK)
+        q = jnp.dot(t[...], wcol[...], preferred_element_type=F32)
         hi = q.astype(BF16)
         qh[part] = hi
         ql[part] = (q - hi.astype(F32)).astype(BF16)
+
+    load(0).wait()
+    transmit(0, t0)
+    for i in range(1, chunks):
+        load(i).wait()
+
+    @pl.loop(0, chunks // 2 - 1)
+    def _(k):
+        transmit(2 * k + 1, t1)
+        contract(2 * k, t0)
+        transmit(2 * k + 2, t0)
+        contract(2 * k + 1, t1)
+
+    transmit(chunks - 1, t1)
+    contract(chunks - 2, t0)
+    contract(chunks - 1, t1)
 
     pl.semaphore_wait(barrier, CHIPS)
     give = pltpu.make_async_remote_copy(
@@ -280,12 +300,11 @@
     @pl.loop(0, 2)
     def _(d):
         re, im = across(seq, 2 * d, cols), across(seq, 2 * d + 1, cols)
-        upper = pl.ds(pl.multiple_of(256 * d, 128), 128)
-        lower = pl.ds(pl.multiple_of(256 * d + 128, 128), 128)
-        wb_ref[upper, :cols] = re
-        wb_ref[upper, cols:] = im
-        wb_ref[lower, :cols] = -im
-        wb_ref[lower, cols:] = re
+        part = pl.ds(pl.multiple_of(128 * d, 128), 128)
+        re32, im32 = re.astype(F32), im.astype(F32)
+        wb_ref[0, part] = re
+        wb_ref[1, part] = (im32 - re32).astype(BF16)
+        wb_ref[2, part] = (im32 + re32).astype(BF16)
 
     pltpu.make_async_copy(mine.at[everything], mine.at[everything], ag_recv).wait()
     show = pltpu.make_async_remote_copy(
@@ -304,41 +323,76 @@
     show.wait_send()
 
 
-def backward_kernel(factor, field_in, target, at, wb, dtr, dti, grad_ref, field_out, v_ref, g_ref):
+def backward_kernel(
+    factor,
+    field_in,
+    target,
+    at,
+    wb,
+    dtr,
+    dti,
+    grad_hbm,
+    field_out,
+    g_ref,
+    vr_ref,
+    vi_ref,
+    vs_ref,
+    out,
+    sem,
+):
     rows, cols = dtr.shape
-    i = pl.program_id(0)
-
-    @pl.when(i == 0)
-    def _():
+    blocks = rows // MROWS
+    for d in range(2):
+        for p in range(CHIPS):
+            lo = 4 * p
+            field_out[d, lo // 128, lo % 128 : lo % 128 + 4, :] = field_in[d, p]
+        fr, fi = field_out[d, 0], field_out[d, 1]
+        excess = 4.0 * factor * (fr * fr + fi * fi - target[d])
+        gr, gi = excess * fr, excess * fi
+        g_ref[d] = jnp.concatenate(
+            [jnp.concatenate([gr, -gi], axis=1), jnp.concatenate([gi, gr], axis=1)], axis=0
+        ).astype(BF16)
+
+    @pl.loop(0, blocks)
+    def _(j):
+        part = pl.ds(pl.multiple_of(j * MROWS, MROWS), MROWS)
         for d in range(2):
-            for p in range(CHIPS):
-                lo = 4 * p
-                field_out[d, lo // 128, lo % 128 : lo % 128 + 4, :] = field_in[d, p]
-            fr, fi = field_out[d, 0], field_out[d, 1]
-            excess = 4.0 * factor * (fr * fr + fi * fi - target[d])
-            gr, gi = excess * fr, excess * fi
-            g_ref[d] = jnp.concatenate(
-                [jnp.concatenate([gr, -gi], axis=1), jnp.concatenate([gi, gr], axis=1)], axis=0
-            ).astype(BF16)
-
-        @pl.loop(0, rows // MROWS)
-        def _(j):
-            part = pl.ds(pl.multiple_of(j * MROWS, MROWS), MROWS)
-            for d in range(2):
-                v = jnp.dot(
-                    at[part, 256 * d : 256 * d + 256], g_ref[d], preferred_element_type=F32
-                )
-                v_ref[part, 256 * d : 256 * d + 256] = v.astype(BF16)
-
-    height = grad_ref.shape[0]
-    part = pl.ds(pl.multiple_of(i * height, height), height)
-    v = v_ref[part, :]
-    for n in range(cols // 256):
-        left = slice(n * 256, (n + 1) * 256)
-        right = slice(cols + n * 256, cols + (n + 1) * 256)
-        hr = jnp.dot(v, wb[:, left], preferred_element_type=F32)
-        hi = jnp.dot(v, wb[:, right], preferred_element_type=F32)
-        grad_ref[:, left] = dtr[part, left] * hr - dti[part, left] * hi
+            v = jnp.dot(at[part, 256 * d : 256 * d + 256], g_ref[d], preferred_element_type=F32)
+            v = v.astype(BF16)
+            lanes = slice(128 * d, 128 * d + 128)
+            vr_ref[part, lanes] = v[:, :128]
+            vi_ref[part, lanes] = v[:, 128:]
+            vs_ref[part, lanes] = (v[:, :128].astype(F32) + v[:, 128:].astype(F32)).astype(BF16)
+
+    def write(i, n):
+        slot = lax.rem(i, 2)
+        lanes = pl.ds(n * 256, 256)
+        return pltpu.make_async_copy(
+            out.at[slot, :, lanes],
+            grad_hbm.at[pl.ds(pl.multiple_of(i * MROWS, MROWS), MROWS), lanes],
+            sem.at[slot, n],
+        )
+
+    @pl.loop(0, blocks)
+    def _(i):
+        @pl.when(i >= 2)
+        def _():
+            for n in range(cols // 256):
+                write(i - 2, n).wait()
+
+        part = pl.ds(pl.multiple_of(i * MROWS, MROWS), MROWS)
+        slot = lax.rem(i, 2)
+        for n in range(cols // 256):
+            lanes = slice(n * 256, (n + 1) * 256)
+            k1 = jnp.dot(vs_ref[part, :], wb[0, :, lanes], preferred_element_type=F32)
+            k2 = jnp.dot(vr_ref[part, :], wb[1, :, lanes], preferred_element_type=F32)
+            k3 = jnp.dot(vi_ref[part, :], wb[2, :, lanes], preferred_element_type=F32)
+            out[slot, :, lanes] = dtr[part, lanes] * (k1 - k3) - dti[part, lanes] * (k1 + k2)
+            write(i, n).start()
+
+    for i in range(blocks - 2, blocks):
+        for n in range(cols // 256):
+            write(i, n).wait()
 
 
 def body(design, coefficients, focal_steps, target):
@@ -346,7 +400,6 @@
     total = rows * lax.axis_size("row")
     focal = target.shape[1]
     vmem = pl.BlockSpec(memory_space=pltpu.VMEM)
-    smem = pl.BlockSpec(memory_space=pltpu.SMEM)
     dma = pltpu.SemaphoreType.DMA
     field, dtr, dti, at, wb, target = pl.pallas_call(
         functools.partial(forward_kernel, total),
@@ -355,14 +408,17 @@
             pltpu.VMEM((rows, cols), F32),
             pltpu.VMEM((rows, cols), F32),
             pltpu.VMEM((rows, 512), BF16),
-            pltpu.VMEM((512, 2 * cols), BF16),
+            pltpu.VMEM((3, 256, cols), BF16),
             pltpu.VMEM(target.shape, F32),
         ),
-        in_specs=[pl.BlockSpec(memory_space=pl.ANY), smem, smem, pl.BlockSpec(memory_space=pl.ANY)],
+        in_specs=[pl.BlockSpec(memory_space=pltpu.HBM)] * 4,
         out_specs=(vmem,) * 6,
         scratch_shapes=[
+            pltpu.SMEM(coefficients.shape, F32),
+            pltpu.SMEM(focal_steps.shape, jnp.int32),
             pltpu.VMEM((rows, cols), F32),
-            pltpu.VMEM((rows, 2 * cols), BF16),
+            pltpu.VMEM((CHUNK, 2 * cols), BF16),
+            pltpu.VMEM((CHUNK, 2 * cols), BF16),
             pltpu.VMEM((2 * cols, 512), BF16),
             pltpu.VMEM((512, rows), BF16),
             pltpu.VMEM((rows, 512), BF16),
@@ -372,7 +428,7 @@
             pltpu.VMEM((256, 128), F32),
             pltpu.VMEM((CHIPS, 4, 128), F32),
             pltpu.VMEM((CHIPS, 4, 128), F32),
-            dma((rows // CHUNK + 1,)),
+            dma((rows // CHUNK + 3,)),
             dma((2,)),
             dma((2,)),
             dma,
@@ -384,23 +440,25 @@
             collective_id=0, has_side_effects=True, vmem_limit_bytes=30 * 2**20
         ),
         name="forward",
-    )(design, coefficients, focal_steps, target)
+    )(*(pltpu.with_memory_space_constraint(a, pltpu.HBM) for a in (design, coefficients, focal_steps, target)))
 
     factor = math.sqrt(total * total) / (4.0 * focal)
-    height = MROWS
     gradient, field = pl.pallas_call(
         functools.partial(backward_kernel, factor),
-        grid=(rows // height,),
         out_shape=(
             jax.ShapeDtypeStruct((rows, cols), F32),
             jax.ShapeDtypeStruct((2, 2, focal, focal), F32),
         ),
         in_specs=[vmem] * 6,
-        out_specs=(
-            pl.BlockSpec((height, cols), lambda i: (i, 0)),
-            pl.BlockSpec((2, 2, focal, focal), lambda i: (0, 0, 0, 0)),
-        ),
-        scratch_shapes=[pltpu.VMEM((rows, 512), BF16), pltpu.VMEM((2, 256, 256), BF16)],
+        out_specs=(pl.BlockSpec(memory_space=pl.ANY), vmem),
+        scratch_shapes=[
+            pltpu.VMEM((2, 256, 256), BF16),
+            pltpu.VMEM((rows, 256), BF16),
+            pltpu.VMEM((rows, 256), BF16),
+            pltpu.VMEM((rows, 256), BF16),
+            pltpu.VMEM((2, MROWS, cols), F32),
+            dma((2, cols // 256)),
+        ],
         compiler_params=pltpu.CompilerParams(vmem_limit_bytes=14 * 2**20),
         name="backward",
     )(field, target, at, wb, dtr, dti)

time: 50.6 us -> 43 us (0.85)
  Pallas kernels: 47.5 us -> 42.3 us
  local copies, waits for them, and re-layouts: 2.23 us -> 0 us
    pallas_call x1, Pallas kernels: 39.8 us -> 35.4 us  [body(): pl.pallas_call(functools.partial(forward_kernel, total), out_shape=(pltpu...]
    unnamed x6 -> x0, local copies, waits for them, and re-layouts: 2.23 us -> none
    pallas_call x1, Pallas kernels: 7.76 us -> 6.88 us  [body(): pl.pallas_call(functools.partial(backward_kernel, factor), out_shape=(jax...]
where the time goes in v3:
time: 43 us; the launch traced here: 42.9 us
  Pallas kernels  42.3 us (98%)
  between operations  0.64 us (1%)
    pallas_call x1, Pallas kernels, body(): pl.pallas_call(functools.partial(forward_kernel, total), out_shape=(pltpu...  35.4 us
    pallas_call x1, Pallas kernels, body(): pl.pallas_call(functools.partial(backward_kernel, factor), out_shape=(jax...  6.88 us

profile of v3, /device:TPU:1, one launch (start us, length us, event | category | flops | bytes accessed | tf_op | source)
XLA Modules:
  0.0 42.9 jit_solution(3932923488961308743)
XLA Ops:
  0.6 35.4 %forward.1 = (f32[2,64,4,128]{3,2,1,0:T(4,128)S(1)}, f32[2048,1024]{1,0:T(8,128)S(1)}, f32[2048,1024]{1,0:T(8,128)S(1)}, bf16[2048,512]{1,0:T(8,128)(2,1)S(1)}, ...) custom-call(f32[2048,1024]{1,0:T(8,128)} %design_hbm.1, f32[2,8]{1,0:T(2,128)} %coef_hbm.1, s32[2]{0:T(128)} %steps_hbm.1, ...), custom_call_target="tpu_custom_call" | custom-call | tf_op jit(solution)/shard_map/forward/pallas_call | solution.py:404
  36.1 6.9 %backward.1 = (f32[2048,1024]{1,0:T(8,128)}, f32[2,2,128,128]{3,2,1,0:T(8,128)}) custom-call(f32[2,64,4,128]{3,2,1,0:T(4,128)S(1)} %get-tuple-element.8.field_in, f32[2,128,128]{2,1,0:T(8,128)S(1)} %get-tuple-element.9.target, bf16[2048,512]{1,0:T(8,128)(2,1)S(1)} %get-tuple-element.10.at, bf16[3,256,1024]{2,1,0:T(8,128)(2,1)S(1)} %get-tuple-element.11.wb, ...), custom_call_target="tpu_custom_call" | custom-call | tf_op jit(solution)/shard_map/backward/pallas_call | solution.py:446

commit v4 on v3

--- a/solution.py
+++ b/solution.py
@@ -95,12 +95,17 @@
     coef_hbm,
     steps_hbm,
     target_hbm,
-    field_ref,
+    field_out,
     dtr_ref,
     dti_ref,
-    at_ref,
+    vr_ref,
+    vi_ref,
+    vs_ref,
     wb_ref,
     target_ref,
+    field_ref,
+    at_ref,
+    g_ref,
     coef,
     steps,
     x_ref,
@@ -109,8 +114,8 @@
     wcol,
     rtab,
     qh,
-    ql,
     seq,
+    row_seq,
     partial,
     sib,
     pieces,
@@ -172,6 +177,7 @@
     mono = [monomials([coef[i, k] for k in range(8)]) for i in range(2)]
 
     seq[:, : cols + 128] = chirp_rows(-first_col - cols, cols + 128, total, step)
+    row_seq[...] = chirp_rows(first_row - 128, rows + 128, total, step)
 
     @pl.loop(0, cols // 128)
     def _(b):
@@ -185,11 +191,8 @@
             wcol[lower, 256 * d : 256 * d + 128] = -im
             wcol[lower, 256 * d + 128 : 256 * d + 256] = re
 
-    seq[...] = chirp_rows(first_row - 128, rows + 128, total, step)
-
-    @pl.loop(0, 4)
-    def _(r):
-        rtab[pl.ds(pl.multiple_of(128 * r, 128), 128), :] = across(seq, r, rows)
+    def row_table(r):
+        rtab[pl.ds(pl.multiple_of(128 * r, 128), 128), :] = across(row_seq, r, rows)
 
     def transmit(i, t):
         v = x_ref[pl.ds(pl.multiple_of(i * CHUNK, CHUNK), CHUNK)]
@@ -199,9 +202,7 @@
     def contract(i, t):
         part = pl.ds(pl.multiple_of(i * CHUNK, CHUNK), CHUNK)
         q = jnp.dot(t[...], wcol[...], preferred_element_type=F32)
-        hi = q.astype(BF16)
-        qh[part] = hi
-        ql[part] = (q - hi.astype(F32)).astype(BF16)
+        qh[part] = q.astype(BF16)
 
     load(0).wait()
     transmit(0, t0)
@@ -210,11 +211,13 @@
 
     @pl.loop(0, chunks // 2 - 1)
     def _(k):
+        row_table(k)
         transmit(2 * k + 1, t1)
         contract(2 * k, t0)
         transmit(2 * k + 2, t0)
         contract(2 * k + 1, t1)
 
+    row_table(3)
     transmit(chunks - 1, t1)
     contract(chunks - 2, t0)
     contract(chunks - 1, t1)
@@ -234,9 +237,7 @@
         d = other + i * (2 * core - 1)
         a = rtab[pl.ds(pl.multiple_of(d * 256, 256), 256), :]
         lanes = pl.ds(pl.multiple_of(d * 256, 256), 256)
-        f = jnp.dot(a, qh[:, lanes], preferred_element_type=F32) + jnp.dot(
-            a, ql[:, lanes], preferred_element_type=F32
-        )
+        f = jnp.dot(a, qh[:, lanes], preferred_element_type=F32)
         partial[i, :128] = f[:128, :128] - f[128:, 128:]
         partial[i, 128:] = f[:128, 128:] + f[128:, :128]
 
@@ -316,7 +317,37 @@
         device_id_type=MESH,
     )
     show.start()
-    show.wait_recv()
+
+    factor = math.sqrt(total * total) / (4.0 * 128)
+
+    @pl.loop(0, 2)
+    def _(i):
+        d = core + i * (1 - 2 * core)
+
+        @pl.when(i == 1)
+        def _():
+            show.wait_recv()
+
+        for p in range(CHIPS):
+            lo = 4 * p
+            field_out[d, lo // 128, lo % 128 : lo % 128 + 4, :] = field_ref[d, p]
+        fr, fi = field_out[d, 0], field_out[d, 1]
+        excess = 4.0 * factor * (fr * fr + fi * fi - target_ref[d])
+        gr, gi = excess * fr, excess * fi
+        g_ref[...] = jnp.concatenate(
+            [jnp.concatenate([gr, -gi], axis=1), jnp.concatenate([gi, gr], axis=1)], axis=0
+        ).astype(BF16)
+        near = pl.ds(pl.multiple_of(256 * d, 256), 256)
+        lanes = pl.ds(pl.multiple_of(128 * d, 128), 128)
+
+        @pl.loop(0, rows // MROWS)
+        def _(j):
+            part = pl.ds(pl.multiple_of(j * MROWS, MROWS), MROWS)
+            v = jnp.dot(at_ref[part, near], g_ref[...], preferred_element_type=F32).astype(BF16)
+            vr_ref[part, lanes] = v[:, :128]
+            vi_ref[part, lanes] = v[:, 128:]
+            vs_ref[part, lanes] = (v[:, :128].astype(F32) + v[:, 128:].astype(F32)).astype(BF16)
+
     give.wait_send()
     pltpu.make_async_copy(landed.at[everything], landed.at[everything], rs_send).wait()
     pltpu.make_async_copy(landed.at[everything], landed.at[everything], ag_send).wait()
@@ -324,45 +355,12 @@
 
 
 def backward_kernel(
-    factor,
-    field_in,
-    target,
-    at,
-    wb,
-    dtr,
-    dti,
-    grad_hbm,
-    field_out,
-    g_ref,
-    vr_ref,
-    vi_ref,
-    vs_ref,
-    out,
-    sem,
+    field, vr_ref, vi_ref, vs_ref, wb, dtr, dti, grad_hbm, field_hbm, out, sem, field_sem
 ):
     rows, cols = dtr.shape
     blocks = rows // MROWS
-    for d in range(2):
-        for p in range(CHIPS):
-            lo = 4 * p
-            field_out[d, lo // 128, lo % 128 : lo % 128 + 4, :] = field_in[d, p]
-        fr, fi = field_out[d, 0], field_out[d, 1]
-        excess = 4.0 * factor * (fr * fr + fi * fi - target[d])
-        gr, gi = excess * fr, excess * fi
-        g_ref[d] = jnp.concatenate(
-            [jnp.concatenate([gr, -gi], axis=1), jnp.concatenate([gi, gr], axis=1)], axis=0
-        ).astype(BF16)
-
-    @pl.loop(0, blocks)
-    def _(j):
-        part = pl.ds(pl.multiple_of(j * MROWS, MROWS), MROWS)
-        for d in range(2):
-            v = jnp.dot(at[part, 256 * d : 256 * d + 256], g_ref[d], preferred_element_type=F32)
-            v = v.astype(BF16)
-            lanes = slice(128 * d, 128 * d + 128)
-            vr_ref[part, lanes] = v[:, :128]
-            vi_ref[part, lanes] = v[:, 128:]
-            vs_ref[part, lanes] = (v[:, :128].astype(F32) + v[:, 128:].astype(F32)).astype(BF16)
+    show = pltpu.make_async_copy(field, field_hbm, field_sem)
+    show.start()
 
     def write(i, n):
         slot = lax.rem(i, 2)
@@ -393,6 +391,7 @@
     for i in range(blocks - 2, blocks):
         for n in range(cols // 256):
             write(i, n).wait()
+    show.wait()
 
 
 def body(design, coefficients, focal_steps, target):
@@ -401,19 +400,25 @@
     focal = target.shape[1]
     vmem = pl.BlockSpec(memory_space=pltpu.VMEM)
     dma = pltpu.SemaphoreType.DMA
-    field, dtr, dti, at, wb, target = pl.pallas_call(
+    half = pltpu.VMEM((rows, 256), BF16)
+    field, dtr, dti, vr, vi, vs, wb = pl.pallas_call(
         functools.partial(forward_kernel, total),
         out_shape=(
-            pltpu.VMEM((2, CHIPS, 4, 128), F32),
+            pltpu.VMEM((2, 2, focal, focal), F32),
             pltpu.VMEM((rows, cols), F32),
             pltpu.VMEM((rows, cols), F32),
-            pltpu.VMEM((rows, 512), BF16),
+            half,
+            half,
+            half,
             pltpu.VMEM((3, 256, cols), BF16),
-            pltpu.VMEM(target.shape, F32),
         ),
         in_specs=[pl.BlockSpec(memory_space=pltpu.HBM)] * 4,
-        out_specs=(vmem,) * 6,
+        out_specs=(vmem,) * 7,
         scratch_shapes=[
+            pltpu.VMEM(target.shape, F32),
+            pltpu.VMEM((2, CHIPS, 4, 128), F32),
+            pltpu.VMEM((rows, 512), BF16),
+            pltpu.VMEM((256, 256), BF16),
             pltpu.SMEM(coefficients.shape, F32),
             pltpu.SMEM(focal_steps.shape, jnp.int32),
             pltpu.VMEM((rows, cols), F32),
@@ -422,7 +427,7 @@
             pltpu.VMEM((2 * cols, 512), BF16),
             pltpu.VMEM((512, rows), BF16),
             pltpu.VMEM((rows, 512), BF16),
-            pltpu.VMEM((rows, 512), BF16),
+            pltpu.VMEM((8, rows + 128), F32),
             pltpu.VMEM((8, rows + 128), F32),
             pltpu.VMEM((2, 256, 128), F32),
             pltpu.VMEM((256, 128), F32),
@@ -442,26 +447,23 @@
         name="forward",
     )(*(pltpu.with_memory_space_constraint(a, pltpu.HBM) for a in (design, coefficients, focal_steps, target)))
 
-    factor = math.sqrt(total * total) / (4.0 * focal)
+    anywhere = pl.BlockSpec(memory_space=pl.ANY)
     gradient, field = pl.pallas_call(
-        functools.partial(backward_kernel, factor),
+        backward_kernel,
         out_shape=(
             jax.ShapeDtypeStruct((rows, cols), F32),
             jax.ShapeDtypeStruct((2, 2, focal, focal), F32),
         ),
-        in_specs=[vmem] * 6,
-        out_specs=(pl.BlockSpec(memory_space=pl.ANY), vmem),
+        in_specs=[vmem] * 7,
+        out_specs=(anywhere, anywhere),
         scratch_shapes=[
-            pltpu.VMEM((2, 256, 256), BF16),
-            pltpu.VMEM((rows, 256), BF16),
-            pltpu.VMEM((rows, 256), BF16),
-            pltpu.VMEM((rows, 256), BF16),
             pltpu.VMEM((2, MROWS, cols), F32),
             dma((2, cols // 256)),
+            dma,
         ],
-        compiler_params=pltpu.CompilerParams(vmem_limit_bytes=14 * 2**20),
+        compiler_params=pltpu.CompilerParams(vmem_limit_bytes=10 * 2**20),
         name="backward",
-    )(field, target, at, wb, dtr, dti)
+    )(field, vr, vi, vs, wb, dtr, dti)
     return gradient, field
 
 

time: 43 us -> 41.1 us (0.956)
  Pallas kernels: 42.3 us -> 40.3 us
    pallas_call x1, Pallas kernels: 6.88 us -> 4.92 us  [body(): pl.pallas_call(backward_kernel, out_shape=(jax.ShapeDtypeStruct((rows, co...]
where the time goes in v4:
time: 41.1 us; the launch traced here: 41 us
  Pallas kernels  40.3 us (98%)
  between operations  0.64 us (2%)
    pallas_call x1, Pallas kernels, body(): pl.pallas_call(functools.partial(forward_kernel, total), out_shape=(pltpu...  35.4 us
    pallas_call x1, Pallas kernels, body(): pl.pallas_call(backward_kernel, out_shape=(jax.ShapeDtypeStruct((rows, co...  4.92 us

profile of v4, /device:TPU:1, one launch (start us, length us, event | category | flops | bytes accessed | tf_op | source)
XLA Modules:
  0.0 41.0 jit_solution(6534712601107039108)
XLA Ops:
  0.6 35.4 %forward.1 = (f32[2,2,128,128]{3,2,1,0:T(8,128)S(1)}, f32[2048,1024]{1,0:T(8,128)S(1)}, f32[2048,1024]{1,0:T(8,128)S(1)}, bf16[2048,256]{1,0:T(8,128)(2,1)S(1)},...) custom-call(f32[2048,1024]{1,0:T(8,128)} %design_hbm.1, ...), custom_call_target="tpu_custom_call" | custom-call | tf_op jit(solution)/shard_map/forward/pallas_call | solution.py:404
  36.0 4.9 %backward.1 = (f32[2048,1024]{1,0:T(8,128)}, f32[2,2,128,128]{3,2,1,0:T(8,128)}) custom-call(f32[2,2,128,128]{3,2,1,0:T(8,128)S(1)} %get-tuple-element.9.field, bf16[2048,256]{1,0:T(8,128)(2,1)S(1)} %get-tuple-element.10.vr_ref, bf16[2048,256]{1,0:T(8,128)(2,1)S(1)} %get-tuple-element.11.vi_ref, bf16[2048,256]{1,0:T(8,128)(2,1)S(1)} %get-tuple-element.12.vs_ref, ...), custom_call_target="tpu_custom_call" | custom-call | tf_op jit(solution)/shard_map/backward/pallas_call | solution.py:451

commit v5 on v4

--- a/solution.py
+++ b/solution.py
@@ -13,7 +13,7 @@
 AXIS = 4
 CHIPS = 64
 CHUNK = 256
-MROWS = 512
+MROWS = 1024
 
 
 def hops(off):
@@ -81,11 +81,6 @@
 
 def across(seq, r, width):
     x = jnp.broadcast_to(seq[pl.ds(r, 1), : width + 128], (128, width + 128))
-    return pltpu.roll(x, 0, 1, stride=1, stride_axis=0)[:, 128:].astype(BF16)
-
-
-def down(seq, r, lo):
-    x = jnp.broadcast_to(seq[r : r + 1, pl.ds(pl.multiple_of(lo, 128), 256)], (128, 256))
     return pltpu.roll(x, 0, 1, stride=1, stride_axis=0)[:, 128:].astype(BF16)
 
 
@@ -177,19 +172,20 @@
     mono = [monomials([coef[i, k] for k in range(8)]) for i in range(2)]
 
     seq[:, : cols + 128] = chirp_rows(-first_col - cols, cols + 128, total, step)
-    row_seq[...] = chirp_rows(first_row - 128, rows + 128, total, step)
-
-    @pl.loop(0, cols // 128)
-    def _(b):
-        upper = pl.ds(pl.multiple_of(b * 128, 128), 128)
-        lower = pl.ds(pl.multiple_of(cols + b * 128, 128), 128)
-        lo = cols - 128 - b * 128
-        for d in range(2):
-            re, im = down(seq, 2 * d, lo), down(seq, 2 * d + 1, lo)
-            wcol[upper, 256 * d : 256 * d + 128] = re
-            wcol[upper, 256 * d + 128 : 256 * d + 256] = im
-            wcol[lower, 256 * d : 256 * d + 128] = -im
-            wcol[lower, 256 * d + 128 : 256 * d + 256] = re
+
+    @pl.loop(0, 2)
+    def _(d):
+        re, im = across(seq, 2 * d, cols), across(seq, 2 * d + 1, cols)
+        left = pl.ds(pl.multiple_of(256 * d, 128), 128)
+        right = pl.ds(pl.multiple_of(256 * d + 128, 128), 128)
+        for b in range(cols // 128):
+            lo = cols - 128 - b * 128
+            upper = slice(b * 128, b * 128 + 128)
+            lower = slice(cols + b * 128, cols + b * 128 + 128)
+            wcol[upper, left] = re[:, lo : lo + 128]
+            wcol[upper, right] = im[:, lo : lo + 128]
+            wcol[lower, left] = -im[:, lo : lo + 128]
+            wcol[lower, right] = re[:, lo : lo + 128]
 
     def row_table(r):
         rtab[pl.ds(pl.multiple_of(128 * r, 128), 128), :] = across(row_seq, r, rows)
@@ -205,18 +201,19 @@
         qh[part] = q.astype(BF16)
 
     load(0).wait()
+    row_seq[...] = chirp_rows(first_row - 128, rows + 128, total, step)
     transmit(0, t0)
-    for i in range(1, chunks):
-        load(i).wait()
-
     @pl.loop(0, chunks // 2 - 1)
     def _(k):
+        load(2 * k + 1).wait()
+        load(2 * k + 2).wait()
         row_table(k)
         transmit(2 * k + 1, t1)
         contract(2 * k, t0)
         transmit(2 * k + 2, t0)
         contract(2 * k + 1, t1)
 
+    load(chunks - 1).wait()
     row_table(3)
     transmit(chunks - 1, t1)
     contract(chunks - 2, t0)
@@ -263,18 +260,21 @@
 
     slopes = [[k * m[k] for k in range(1, 8)] for m in mono]
 
-    @pl.loop(0, rows // 32)
-    def _(i):
+    def slope(i):
         part = pl.ds(pl.multiple_of(i * 32, 32), 32)
         v = x_ref[part]
         dtr_ref[part] = horner(v, slopes[0])
         dti_ref[part] = horner(v, slopes[1])
 
+    first = rows // 32 * 5 // 8
+    pl.loop(0, first)(slope)
+
     everything = pl.ds(0, CHIPS - 1)
     pltpu.make_async_copy(landed.at[everything], landed.at[everything], rs_recv).wait()
-    total_piece = pieces[chip]
-    for n in range(CHIPS - 1):
-        total_piece = total_piece + landed[n]
+    sums = [pieces[chip]] + [landed[n] for n in range(CHIPS - 1)]
+    while len(sums) > 1:
+        sums = [sums[n] + sums[n + 1] for n in range(0, len(sums), 2)]
+    total_piece = sums[0]
     mine = field_ref.at[core]
     mine[chip] = total_piece
 
@@ -288,13 +288,16 @@
             device_id_type=MESH,
         ).start()
 
+    pl.loop(first, rows // 32)(slope)
     seq[...] = chirp_rows(-first_row - rows, rows + 128, total, step)
 
-    @pl.loop(0, rows // 128)
-    def _(b):
-        part = pl.ds(pl.multiple_of(b * 128, 128), 128)
-        for r in range(4):
-            at_ref[part, 128 * r : 128 * r + 128] = down(seq, r, rows - 128 - b * 128)
+    @pl.loop(0, 4)
+    def _(r):
+        wide = across(seq, r, rows)
+        lanes = pl.ds(pl.multiple_of(128 * r, 128), 128)
+        for b in range(rows // 128):
+            lo = rows - 128 - b * 128
+            at_ref[b * 128 : b * 128 + 128, lanes] = wide[:, lo : lo + 128]
 
     seq[:, : cols + 128] = chirp_rows(first_col - 128, cols + 128, total, step)
 
@@ -461,7 +464,7 @@
             dma((2, cols // 256)),
             dma,
         ],
-        compiler_params=pltpu.CompilerParams(vmem_limit_bytes=10 * 2**20),
+        compiler_params=pltpu.CompilerParams(vmem_limit_bytes=16 * 2**20),
         name="backward",
     )(field, vr, vi, vs, wb, dtr, dti)
     return gradient, field

time: 41.1 us -> 37.2 us (0.905)
  Pallas kernels: 40.3 us -> 36.4 us
    pallas_call x1, Pallas kernels: 35.4 us -> 31.7 us  [body(): pl.pallas_call(functools.partial(forward_kernel, total), out_shape=(pltpu...]
where the time goes in v5:
time: 37.2 us; the launch traced here: 37.1 us
  Pallas kernels  36.4 us (98%)
  between operations  0.64 us (2%)
    pallas_call x1, Pallas kernels, body(): pl.pallas_call(functools.partial(forward_kernel, total), out_shape=(pltpu...  31.7 us
    pallas_call x1, Pallas kernels, body(): pl.pallas_call(backward_kernel, out_shape=(jax.ShapeDtypeStruct((rows, co...  4.75 us

profile of v5, /device:TPU:1, one launch (start us, length us, event | category | flops | bytes accessed | tf_op | source)
XLA Modules:
  0.0 37.1 jit_solution(5772399686991653948)
XLA Ops:
  0.6 31.7 %forward.1 = (f32[2,2,128,128]{3,2,1,0:T(8,128)S(1)}, f32[2048,1024]{1,0:T(8,128)S(1)}, f32[2048,1024]{1,0:T(8,128)S(1)}, bf16[2048,256]{1,0:T(8,128)(2,1)S(1)},...) custom-call(f32[2048,1024]{1,0:T(8,128)} %design_hbm.1, ...), custom_call_target="tpu_custom_call" | custom-call | tf_op jit(solution)/shard_map/forward/pallas_call | solution.py:407
  32.3 4.8 %backward.1 = (f32[2048,1024]{1,0:T(8,128)}, f32[2,2,128,128]{3,2,1,0:T(8,128)}) custom-call(f32[2,2,128,128]{3,2,1,0:T(8,128)S(1)} %get-tuple-element.9.field, bf16[2048,256]{1,0:T(8,128)(2,1)S(1)} %get-tuple-element.10.vr_ref, bf16[2048,256]{1,0:T(8,128)(2,1)S(1)} %get-tuple-element.11.vi_ref, bf16[2048,256]{1,0:T(8,128)(2,1)S(1)} %get-tuple-element.12.vs_ref, ...), custom_call_target="tpu_custom_call" | custom-call | tf_op jit(solution)/shard_map/backward/pallas_call | solution.py:454

commit v6 on v5

--- a/solution.py
+++ b/solution.py
@@ -28,7 +28,7 @@
         for c in range(AXIS)
         if (a, b, c) != (0, 0, 0)
     ),
-    key=lambda off: -hops(off),
+    key=lambda off: (-hops(off), off[::-1]),
 )
 
 

time: 37.2 us -> 37.2 us (level)
  no operation moved by 1% of the time
where the time goes in v6:
time: 37.2 us; the launch traced here: 37.1 us
  Pallas kernels  36.4 us (98%)
  between operations  0.64 us (2%)
    pallas_call x1, Pallas kernels, body(): pl.pallas_call(functools.partial(forward_kernel, total), out_shape=(pltpu...  31.7 us
    pallas_call x1, Pallas kernels, body(): pl.pallas_call(backward_kernel, out_shape=(jax.ShapeDtypeStruct((rows, co...  4.76 us

profile of v6, /device:TPU:1, one launch (start us, length us, event | category | flops | bytes accessed | tf_op | source)
XLA Modules:
  0.0 37.1 jit_solution(3271473861656072530)
XLA Ops:
  0.6 31.7 %forward.1 = (f32[2,2,128,128]{3,2,1,0:T(8,128)S(1)}, f32[2048,1024]{1,0:T(8,128)S(1)}, f32[2048,1024]{1,0:T(8,128)S(1)}, bf16[2048,256]{1,0:T(8,128)(2,1)S(1)},...) custom-call(f32[2048,1024]{1,0:T(8,128)} %design_hbm.1, ...), custom_call_target="tpu_custom_call" | custom-call | tf_op jit(solution)/shard_map/forward/pallas_call | solution.py:407
  32.3 4.8 %backward.1 = (f32[2048,1024]{1,0:T(8,128)}, f32[2,2,128,128]{3,2,1,0:T(8,128)}) custom-call(f32[2,2,128,128]{3,2,1,0:T(8,128)S(1)} %get-tuple-element.9.field, bf16[2048,256]{1,0:T(8,128)(2,1)S(1)} %get-tuple-element.10.vr_ref, bf16[2048,256]{1,0:T(8,128)(2,1)S(1)} %get-tuple-element.11.vi_ref, bf16[2048,256]{1,0:T(8,128)(2,1)S(1)} %get-tuple-element.12.vs_ref, ...), custom_call_target="tpu_custom_call" | custom-call | tf_op jit(solution)/shard_map/backward/pallas_call | solution.py:454
